TPU v7x, 256 devices: a whole 4x4x8 slice. The times are simulated.
256 devices in a mesh: pair: 2 (over y_lo), seq: 16 (over y_hi, z), dp: 8 (over x, core).
Axes of the slice: x: 4, y: 4 (y_hi: 2, y_lo: 2; y = y_hi * 2 + y_lo), z: 8, core: 2. Of those that a mesh axis runs over, the one named last changes fastest.
Arguments:
- latents: bfloat16 [8, 2, 1536, 64], P('dp', 'pair', 'seq'), may hold values from -6 to 6
- noise: bfloat16 [8, 1536, 64], P('dp', 'seq'), may hold values from -6 to 6
- pair_timestep_index: int32 [8], P('dp'), may hold values from 0 to 999
- preferred_image_slot: int32 [8], P('dp'), may hold values from 0 to 1
- prompt_token_states: bfloat16 [8, 512, 3072], P('dp', 'seq'), may hold values from -6 to 6
- image_embed_weight: bfloat16 [64, 3072], replicated, may hold values from -0.75 to 0.75
- timestep_modulation_weight: bfloat16 [256, 18432], P(None, 'seq'), may hold values from -0.375 to 0.375
- image_query_key_value: bfloat16 [3072, 16, 384], P(None, 'seq'), may hold values from -0.109375 to 0.109375
- text_key_value: bfloat16 [3072, 16, 256], P(None, 'seq'), may hold values from -0.109375 to 0.109375
- query_norm_gain: float32 [128], replicated, may hold values from 0.1 to 1.9
- key_norm_gain: float32 [128], replicated, may hold values from 0.1 to 1.9
- adapter_down_weight: bfloat16 [3072, 64], replicated, may hold values from -0.109375 to 0.109375
- adapter_up_weight: bfloat16 [64, 2048], replicated, may hold values from -0.75 to 0.75
- image_output_weight: bfloat16 [2048, 3072], P('seq'), may hold values from -1.25 to 1.25
- latent_out_weight: bfloat16 [3072, 64], replicated, may hold values from -0.109375 to 0.109375
Outputs:
- grad_down: float32 [3072, 64], replicated
- grad_up: float32 [64, 2048], replicated
- pair_loss: float32 [8], P('dp')
All inputs are finite; a program needn't handle non-finite values.
Results may differ from a plain program's by a relative error of at most 0.025.
Values may be sent and summed in bfloat16 or wider, within the bound.
A program may use at most 128 MiB of HBM per device.

v0:
```python
import math

import jax
import jax.numpy as jnp
from jax import lax
from jax.sharding import PartitionSpec as P

epsilon = 1e-06
half_beta = 20.0
horizon = 1000.0


def from_partner(array, axis, apart):
    return lax.ppermute(array, axis, [(i, i ^ 1 << apart) for i in range(lax.axis_size(axis))])


def sinusoid(step_value, width):
    half_width = width // 2
    freqs = jnp.exp(-math.log(10000.0) * jnp.arange(half_width, dtype=jnp.float32) / half_width)
    angle = step_value * freqs
    return jnp.concatenate([jnp.cos(angle), jnp.sin(angle)])


def normalize(states):
    average = jnp.mean(states, -1, keepdims=True)
    centred = states - average
    inv_spread = lax.rsqrt(jnp.mean(centred * centred, -1, keepdims=True) + epsilon)
    return (centred * inv_spread, inv_spread)


def modulated(states, scale_vec, shift_vec):
    return normalize(states)[0] * (1.0 + scale_vec) + shift_vec


def rms_gain(rows, gain):
    return rows * lax.rsqrt(jnp.mean(rows * rows, -1, keepdims=True) + epsilon) * gain


def rms_back(rows, gain, grads):
    inv_root = lax.rsqrt(jnp.mean(rows * rows, -1, keepdims=True) + epsilon)
    weighted = grads * gain
    return inv_root * weighted - rows * inv_root * inv_root * inv_root * jnp.mean(
        rows * weighted, -1, keepdims=True
    )


def norm_back(unit_rows, inv_spread, grads):
    return (
        grads
        - jnp.mean(grads, -1, keepdims=True)
        - unit_rows * jnp.mean(grads * unit_rows, -1, keepdims=True)
    ) * inv_spread


def attend(queries, key_rows, value_rows):
    row_count = queries.shape[0]
    block_rows = math.gcd(row_count, 512)
    inv_root = 1.0 / math.sqrt(queries.shape[2])
    blocks = queries.reshape((row_count // block_rows, block_rows) + queries.shape[1:])

    def one_block(query_block):
        scores = (
            jnp.einsum("qhd,khd->hqk", query_block, key_rows, preferred_element_type=jnp.float32)
            * inv_root
        )
        probs = jax.nn.softmax(scores, axis=-1)
        return jnp.einsum(
            "hqk,khd->qhd",
            probs.astype(jnp.bfloat16),
            value_rows,
            preferred_element_type=jnp.float32,
        ).astype(jnp.bfloat16)

    return lax.map(one_block, blocks).reshape(queries.shape)


def attend_back(queries, key_rows, value_rows, grads):
    row_count = queries.shape[0]
    block_rows = math.gcd(row_count, 512)
    inv_root = 1.0 / math.sqrt(queries.shape[2])
    shaped = (row_count // block_rows, block_rows) + queries.shape[1:]

    def one_block(operands):
        query_block, grad_block = operands
        scores = (
            jnp.einsum("qhd,khd->hqk", query_block, key_rows, preferred_element_type=jnp.float32)
            * inv_root
        )
        probs = jax.nn.softmax(scores, axis=-1)
        g_probs = jnp.einsum(
            "qhd,khd->hqk", grad_block, value_rows, preferred_element_type=jnp.float32
        )
        g_scores = (
            probs * (g_probs - jnp.sum(probs * g_probs, -1, keepdims=True)) * inv_root
        ).astype(jnp.bfloat16)
        return jnp.einsum("hqk,khd->qhd", g_scores, key_rows, preferred_element_type=jnp.float32)

    return lax.map(one_block, (queries.reshape(shaped), grads.reshape(shaped))).reshape(
        queries.shape
    )


def on_device(
    latents,
    noise,
    pair_timestep_index,
    preferred_image_slot,
    prompt_token_states,
    image_embed_weight,
    timestep_modulation_weight,
    image_query_key_value,
    text_key_value,
    query_norm_gain,
    key_norm_gain,
    adapter_down_weight,
    adapter_up_weight,
    image_output_weight,
    latent_out_weight,
):
    seq_count = lax.axis_size("seq")
    pair_count = lax.axis_size("dp")
    my_slot = lax.axis_index("pair")
    img_local = latents.shape[2]
    channels = image_embed_weight.shape[0]
    model_width = image_embed_weight.shape[1]
    heads_here = image_query_key_value.shape[1]
    per_head_width = query_norm_gain.shape[0]
    images = img_local * seq_count
    every_head = adapter_up_weight.shape[1] // per_head_width
    step_value = pair_timestep_index[0].astype(jnp.float32)
    noise_level = (step_value + 1.0) / horizon
    part_mod = jnp.dot(
        sinusoid(step_value, timestep_modulation_weight.shape[0]).astype(jnp.bfloat16)[None],
        timestep_modulation_weight,
        preferred_element_type=jnp.float32,
    )
    modulation = lax.all_gather(part_mod, "seq", axis=1, tiled=True)[0]
    pieces = [
        modulation[part_index * model_width : (part_index + 1) * model_width]
        for part_index in range(6)
    ]
    shift_img, scale_img, shift_txt, scale_txt, shift_out, scale_out = pieces
    latent = latents[0, 0].astype(jnp.float32)
    noise_now = noise[0].astype(jnp.float32)
    noisy = ((1.0 - noise_level) * latent + noise_level * noise_now).astype(jnp.bfloat16)
    target = noise_now - latent
    states = jnp.dot(noisy, image_embed_weight, preferred_element_type=jnp.float32)
    image_rows_normed = modulated(states, scale_img, shift_img).astype(jnp.bfloat16)
    image_matrix = image_query_key_value.reshape(model_width, -1)
    qkv = jnp.dot(
        lax.all_gather(image_rows_normed, "seq", axis=0, tiled=True),
        image_matrix,
        preferred_element_type=jnp.float32,
    ).reshape(-1, heads_here, 3 * per_head_width)
    txt_normed = modulated(prompt_token_states[0].astype(jnp.float32), scale_txt, shift_txt).astype(
        jnp.bfloat16
    )
    text_matrix = text_key_value.reshape(model_width, -1)
    kv_text = jnp.dot(
        lax.all_gather(txt_normed, "seq", axis=0, tiled=True),
        text_matrix,
        preferred_element_type=jnp.float32,
    ).reshape(-1, heads_here, 2 * per_head_width)
    key_rows = jnp.concatenate(
        [
            rms_gain(kv_text[..., :per_head_width], key_norm_gain),
            rms_gain(qkv[..., per_head_width : 2 * per_head_width], key_norm_gain),
        ],
        0,
    ).astype(jnp.bfloat16)
    value_rows = jnp.concatenate(
        [kv_text[..., per_head_width:], qkv[..., 2 * per_head_width :]], 0
    ).astype(jnp.bfloat16)
    rank_projected = jnp.dot(
        image_rows_normed, adapter_down_weight, preferred_element_type=jnp.float32
    ).astype(jnp.bfloat16)
    delta_rows = (
        jnp.dot(rank_projected, adapter_up_weight, preferred_element_type=jnp.float32)
        .astype(jnp.bfloat16)
        .reshape(img_local, every_head, per_head_width)
    )
    query_adapter_change = lax.all_to_all(
        delta_rows, "seq", split_axis=1, concat_axis=0, tiled=True
    )
    q_lin = qkv[..., :per_head_width]
    pol_lin = q_lin + query_adapter_change.astype(jnp.float32)
    q_ref = rms_gain(q_lin, query_norm_gain).astype(jnp.bfloat16)
    q_pol = rms_gain(pol_lin, query_norm_gain).astype(jnp.bfloat16)
    both_out = attend(jnp.concatenate([q_ref, q_pol], 0), key_rows, value_rows)
    out_ref, out_pol = (
        lax.all_to_all(both_out[:images], "seq", split_axis=0, concat_axis=1, tiled=True),
        lax.all_to_all(both_out[images:], "seq", split_axis=0, concat_axis=1, tiled=True),
    )
    projection = lax.all_gather(image_output_weight, "seq", axis=0, tiled=True)
    terms = []
    for heads_out in (out_ref, out_pol):
        mixed = states + jnp.dot(
            heads_out.reshape(img_local, -1), projection, preferred_element_type=jnp.float32
        )
        unit_rows, inv_spread = normalize(mixed)
        normed_out = (unit_rows * (1.0 + scale_out) + shift_out).astype(jnp.bfloat16)
        pred = jnp.dot(normed_out, latent_out_weight, preferred_element_type=jnp.float32)
        diff = target - pred
        terms.append((jnp.sum(diff * diff) / (images * channels), diff, unit_rows, inv_spread))
    err_ref, err_pol = lax.psum((terms[0][0], terms[1][0]), "seq")
    own_gap = err_pol - err_ref
    partner = from_partner(own_gap, "pair", 0)
    winner = preferred_image_slot[0]
    margin = jnp.where(winner == my_slot, own_gap - partner, partner - own_gap)
    pair_value = jax.nn.softplus(half_beta * margin)
    weight_now = jax.nn.sigmoid(half_beta * margin) * half_beta / pair_count
    signed = jnp.where(winner == my_slot, weight_now, -weight_now)
    factor = signed * (-2.0 / (images * channels))
    diff, unit_rows, inv_spread = (terms[1][1], terms[1][2], terms[1][3])
    g_pred = (factor * diff).astype(jnp.bfloat16)
    g_ln = jnp.dot(g_pred, latent_out_weight.T, preferred_element_type=jnp.float32) * (
        1.0 + scale_out
    )
    g_mixed = norm_back(unit_rows, inv_spread, g_ln).astype(jnp.bfloat16)
    g_rows = (
        jnp.dot(g_mixed, projection.T, preferred_element_type=jnp.float32)
        .astype(jnp.bfloat16)
        .reshape(img_local, every_head, per_head_width)
    )
    g_heads = lax.all_to_all(g_rows, "seq", split_axis=1, concat_axis=0, tiled=True)
    g_query = attend_back(q_pol, key_rows, value_rows, g_heads)
    grad_query_change = rms_back(pol_lin, query_norm_gain, g_query).astype(jnp.bfloat16)
    grad_token_rows = lax.all_to_all(
        grad_query_change, "seq", split_axis=0, concat_axis=1, tiled=True
    ).reshape(img_local, -1)
    grad_up_part = jnp.dot(rank_projected.T, grad_token_rows, preferred_element_type=jnp.float32)
    grad_low_rank = jnp.dot(
        grad_token_rows, adapter_up_weight.T, preferred_element_type=jnp.float32
    ).astype(jnp.bfloat16)
    grad_down_part = jnp.dot(image_rows_normed.T, grad_low_rank, preferred_element_type=jnp.float32)
    grad_down, grad_up = lax.psum((grad_down_part, grad_up_part), ("pair", "seq", "dp"))
    return (grad_down, grad_up, pair_value.reshape(1))


def solution(mesh):
    return jax.shard_map(
        on_device,
        mesh=mesh,
        in_specs=(
            P("dp", "pair", "seq", None),
            P("dp", "seq", None),
            P("dp"),
            P("dp"),
            P("dp", "seq", None),
            P(),
            P(None, "seq"),
            P(None, "seq", None),
            P(None, "seq", None),
            P(),
            P(),
            P(),
            P(),
            P("seq", None),
            P(),
        ),
        out_specs=(P(), P(), P("dp")),
        check_vma=False,
    )
```

profile of v0, /device:TPU:1, one launch (start us, length us, event | category | flops | bytes accessed | tf_op | source)
XLA Modules:
  0.0 870.8 jit_solution(11544563982958817292)
XLA Ops:
  9.4 38.0 %all-gather.1 = f32[16,1,1152]{2,1,0:T(1,128)S(1)} all-gather(f32[1,1,1152]{2,1,0:T(1,128)S(1)} %convolution_bitcast_fusion.1), channel_id=2, replica_groups=mesh['pair'=2,'seq'=16,'dp'=8] {'seq'}, dimensions={0}, use_global_device_ids=true | all-gather | bytes 78336 | tf_op jit(solution)/shard_map/all_gather | solution.py:137
  50.2 1.7 fusion.61
  55.7 1.5 convolution_convert_fusion.3
  59.3 4.2 all-to-all-start
  63.5 10.7 %all-to-all-done = bf16[96,16,128]{2,0,1:T(8,128)(2,1)} async-done(((bf16[96,16,128]{2,0,1:T(8,128)(2,1)}), bf16[96,16,128]{2,0,1:T(8,128)(2,1)}, u32[]{:S(2)}, u32[]{:S(2)}) %all-to-all-start) | async-done | bytes 393248 | tf_op jit(solution)/shard_map/all_to_all | solution.py:182
  74.2 2.0 bitcast_convert_fusion
  76.1 68.4 %all-gather.8.cloned.1.call-done = bf16[512,3072]{1,0:T(8,128)(2,1)} async-done(((bf16[32,3072]{1,0:T(8,128)(2,1)}), bf16[512,3072]{1,0:T(8,128)(2,1)}) %all-gather.8.cloned.1.call-update) | async-done | bytes 3145744 | tf_op jit(solution)/shard_map/all_gather | solution.py:160
  144.5 3.3 fusion.35
  149.5 143.6 %all-gather.6.cloned.1.call-done = bf16[1536,3072]{1,0:T(8,128)(2,1)} async-done(((bf16[96,3072]{1,0:T(8,128)(2,1)}), bf16[1536,3072]{1,0:T(8,128)(2,1)}) %all-gather.6.cloned.1.call-update) | async-done | bytes 9437200 | tf_op jit(solution)/shard_map/all_gather | solution.py:151
  293.1 7.5 convolution_bitcast_fusion
  304.8 26.4 %while.20 = (s32[]{:T(128)}, bf16[6,512,1,128]{3,1,2,0:T(8,128)(2,1)}, bf16[6,512,1,128]{3,1,2,0:T(8,128)(2,1)}, bf16[2048,1,128]{2,0,1:T(8,128)(2,1)S(1)}, bf16[2048,1,128]{2,0,1:T(8,128)(2,1)}, /*index=5*/s32[]{:T(128)}) while((s32[]{:T(128)}, bf16[6,512,1,128]{3,1,2,0:T(8,128)(2,1)}, bf16[6,512,1,128]{3,1,2,0:T(8,128)(2,1)}, ...), condition=%wide.region_11.12_spmd, body=%wide.region_8.11_spmd.sunk | while | flops 546372608 | bytes 16002145 | solution.py:74
  304.8 1.7 multiply_reduce_fusion.16
  307.6 1.7 fusion.114
  309.2 1.7 multiply_reduce_fusion.16
  311.9 1.6 fusion.114
  313.6 1.7 multiply_reduce_fusion.16
  316.3 1.6 fusion.114
  318.0 1.7 multiply_reduce_fusion.16
  320.7 1.6 fusion.114
  322.4 1.7 multiply_reduce_fusion.16
  325.1 1.7 fusion.114
  326.8 1.7 multiply_reduce_fusion.16
  329.5 1.7 fusion.114
  334.6 4.2 all-to-all-start.2
  340.4 11.2 %all-to-all-done.2 = bf16[16,2,6144]{2,1,0:T(2,128)(2,1)S(1)} async-done(((bf16[16,2,6144]{2,1,0:T(2,128)(2,1)}), bf16[16,2,6144]{2,1,0:T(2,128)(2,1)S(1)}, u32[]{:S(2)}, u32[]{:S(2)}) %all-to-all-start.2) | async-done | bytes 393248 | tf_op jit(solution)/shard_map/all_to_all | solution.py:191
  351.7 6.4 all-to-all-start.1
  359.4 11.9 %all-to-all-done.1 = bf16[16,2,6144]{2,1,0:T(2,128)(2,1)} async-done(((bf16[16,2,6144]{2,1,0:T(2,128)(2,1)}), bf16[16,2,6144]{2,1,0:T(2,128)(2,1)}, u32[]{:S(2)}, u32[]{:S(2)}) %all-to-all-start.1) | async-done | bytes 393248 | tf_op jit(solution)/shard_map/all_to_all | solution.py:192
  371.2 2.7 reshape.446
  374.9 106.8 %all-gather.10.cloned.1.call-done = bf16[2048,3072]{1,0:T(8,128)(2,1)} async-done(((bf16[128,3072]{1,0:T(8,128)(2,1)}), bf16[2048,3072]{1,0:T(8,128)(2,1)}) %all-gather.10.cloned.1.call-update) | async-done | bytes 12582928 | tf_op jit(solution)/shard_map/all_gather | solution.py:194
  481.8 7.0 fusion.87
  490.0 2.3 fusion.86
  496.1 31.5 %all-reduce.1 = (f32[]{:T(128)}, f32[]{:T(128)}) all-reduce(f32[]{:T(128)S(6)} %div.102, f32[]{:T(128)S(6)} %div.105), channel_id=1, replica_groups=mesh['pair'=2,'seq'=16,'dp'=8] {'seq'}, use_global_device_ids=true, to_apply=%region_15.16 | all-reduce | flops 2 | bytes 16 | tf_op jit(solution)/shard_map/psum | solution.py:205
  529.0 1.9 collective-permute-start
  533.7 8.6 fusion.39
  543.2 4.1 all-to-all-start.3
  547.5 10.4 %all-to-all-done.3 = bf16[96,16,128]{2,0,1:T(8,128)(2,1)S(1)} async-done(((bf16[96,16,128]{2,0,1:T(8,128)(2,1)}), bf16[96,16,128]{2,0,1:T(8,128)(2,1)S(1)}, u32[]{:S(2)}, u32[]{:S(2)}) %all-to-all-start.3) | async-done | bytes 393248 | tf_op jit(solution)/shard_map/all_to_all | solution.py:225
  557.9 15.9 %while.21 = (s32[]{:T(128)}, f32[3,512,1,128]{3,1,2,0:T(8,128)S(1)}, bf16[3,512,1,128]{3,1,2,0:T(8,128)(2,1)S(1)}, bf16[2048,1,128]{2,0,1:T(8,128)(2,1)S(1)}, bf...) while((s32[]{:T(128)}, f32[3,512,1,128]{3,1,2,0:T(8,128)S(1)}, ...), condition=%wide.region_26.27_spmd, body=%wide.region_22.26_spmd.sunk | while | flops 823130624 | bytes 29378676 | solution.py:98
  559.8 1.5 multiply_reduce_fusion.18
  561.3 1.9 fusion.117
  565.1 1.5 multiply_reduce_fusion.18
  566.6 1.9 fusion.117
  570.4 1.5 multiply_reduce_fusion.18
  571.9 1.9 fusion.117
  575.6 14.5 %all_to_all.69 = bf16[16,2,6144]{2,1,0:T(2,128)(2,1)S(1)} all-to-all(bf16[16,2,6144]{2,1,0:T(2,128)(2,1)S(1)} %reshape.449), channel_id=1, replica_groups=mesh['pair'=2,'seq'=16,'dp'=8] {'seq'}, dimensions={0} | all-to-all | bytes 786432 | tf_op jit(solution)/shard_map/all_to_all | solution.py:228
  591.8 2.6 fusion.41
  594.5 264.7 %all-reduce.4.cloned.1.call-done = (f32[3072,64]{0,1:T(8,128)}, f32[64,2048]{1,0:T(8,128)}) async-done(((f32[3072,64]{0,1:T(8,128)}, f32[64,2048]{1,0:T(8,128)}), (f32[3072,64]{0,1:T(8,128)}, f32[64,2048]{1,0:T(8,128)})) %all-reduce.4.cloned.1.call-update) | async-done | bytes 1310736 | tf_op jit(solution)/shard_map/psum | solution.py:236
  859.2 2.1 copy.118
  861.3 1.9 copy.119
  (148 shorter events, 43.4 us)
Async XLA Ops:
  7.2 286.0 %copy-start = (bf16[3072,1,384]{2,0,1:T(8,128)(2,1)S(1)}, bf16[3072,1,384]{2,0,1:T(8,128)(2,1)}, u32[]{:S(2)}) copy-start(bf16[3072,1,384]{2,0,1:T(8,128)(2,1)} %param.26) | copy-start | bytes 7077892
  7.2 137.3 %all-gather.8.cloned.1.call-start = ((), (), s32[]{:S(2)}) async-start(), calls=%async_computation.6 | async-start | bytes 3342336 | tf_op jit(solution)/shard_map/all_gather | solution.py:160
  52.0 241.1 %all-gather.6.cloned.1.call-start = ((), (), s32[]{:S(2)}) async-start(), calls=%async_computation.5 | async-start | bytes 10027008 | tf_op jit(solution)/shard_map/all_gather | solution.py:151
  52.0 1.8 copy-start.14
  55.0 426.8 %all-gather.10.cloned.1.call-start = ((), (), s32[]{:S(2)}) async-start(), calls=%async_computation.7 | async-start | bytes 13369344 | tf_op jit(solution)/shard_map/all_gather | solution.py:194
  59.3 14.9 %all-to-all-start = ((bf16[96,16,128]{2,0,1:T(8,128)(2,1)}), bf16[96,16,128]{2,0,1:T(8,128)(2,1)}, u32[]{:S(2)}, u32[]{:S(2)}) async-start(bf16[96,16,128]{2,0,1:T(8,128)(2,1)} %bitcast.234), calls=%async_computation | async-start | bytes 786432 | tf_op jit(solution)/shard_map/all_to_all | solution.py:182
  144.5 4.2 copy-start.19
  300.7 1.1 copy-start.5
  300.7 1.1 copy-start.18
  300.7 1.1 copy-start.20
  301.2 1.3 copy-start.10
  301.8 0.9 copy-start.9
  302.5 2.3 copy-start.2
  306.5 1.1 copy-start.7
  310.9 1.0 copy-start.7
  315.3 1.0 copy-start.7
  319.7 1.1 copy-start.7
  324.0 1.1 copy-start.7
  328.4 1.1 copy-start.7
  334.6 17.1 %all-to-all-start.2 = ((bf16[16,2,6144]{2,1,0:T(2,128)(2,1)}), bf16[16,2,6144]{2,1,0:T(2,128)(2,1)S(1)}, u32[]{:S(2)}, u32[]{:S(2)}) async-start(bf16[16,2,6144]{2,1,0:T(2,128)(2,1)} %reshape.447), calls=%async_computation.2 | async-start | bytes 786432 | tf_op jit(solution)/shard_map/all_to_all | solution.py:191
  351.7 19.6 %all-to-all-start.1 = ((bf16[16,2,6144]{2,1,0:T(2,128)(2,1)}), bf16[16,2,6144]{2,1,0:T(2,128)(2,1)}, u32[]{:S(2)}, u32[]{:S(2)}) async-start(bf16[16,2,6144]{2,1,0:T(2,128)(2,1)} %reshape.445), calls=%async_computation.1 | async-start | bytes 786432 | tf_op jit(solution)/shard_map/all_to_all | solution.py:192
  481.8 7.3 slice-start
  481.8 7.3 slice-start.1
  481.8 8.2 slice-start.2
  481.8 8.2 copy-start.6
  490.0 2.6 copy-start.11
  490.0 2.7 copy-start.13
  490.0 2.7 copy-start.15
  490.0 2.7 copy-start.16
  490.0 2.7 copy-start.17
  492.3 40.8 %copy-start.12 = (bf16[3072,64]{0,1:T(8,128)(2,1)S(1)}, bf16[3072,64]{0,1:T(8,128)(2,1)}, u32[]{:S(2)}) copy-start(bf16[3072,64]{0,1:T(8,128)(2,1)} %param.33) | copy-start | bytes 1179652
  529.0 2.7 collective-permute-start
  543.2 14.8 %all-to-all-start.3 = ((bf16[96,16,128]{2,0,1:T(8,128)(2,1)}), bf16[96,16,128]{2,0,1:T(8,128)(2,1)S(1)}, u32[]{:S(2)}, u32[]{:S(2)}) async-start(bf16[96,16,128]{2,0,1:T(8,128)(2,1)} %bitcast.201), calls=%async_computation.3 | async-start | bytes 786432 | tf_op jit(solution)/shard_map/all_to_all | solution.py:225
  547.3 311.9 %all-reduce.4.cloned.1.call-start = ((), (), s32[]{:S(2)}) async-start(), calls=%async_computation.8 | async-start | bytes 2621440 | tf_op jit(solution)/shard_map/psum | solution.py:236
  557.9 16.0 %copy-start.3 = (f32[1536,1,128]{2,0,1:T(8,128)S(1)}, f32[1536,1,128]{2,0,1:T(8,128)}, u32[]{:S(2)}) copy-start(f32[1536,1,128]{2,0,1:T(8,128)} %copy-done.2) | copy-start | bytes 2359300
  558.7 1.0 copy-start.8
  564.0 1.0 copy-start.8
  569.3 1.0 copy-start.8
  590.1 1.6 copy-start.4
  591.8 271.4 %copy-start.1 = (bf16[3072,1,384]{2,0,1:T(8,128)(2,1)S(1)}, bf16[3072,1,384]{2,0,1:T(8,128)(2,1)}, u32[]{:S(2)}) copy-start(bf16[3072,1,384]{2,0,1:T(8,128)(2,1)} %param.26) | copy-start | bytes 7077892
Sparse Core Ops, SparseCore 0:
  52.1 92.3 all-gather.7
  147.1 145.9 all-gather.5
  295.7 185.9 all-gather.9
  594.5 264.6 all-reduce.3
where the time goes:
time: 873 us; the launch traced here: 871 us
  waiting for transfers between devices  629 us (72%)
  blocking collectives  84 us (10%)
  matrix products  73.2 us (8%)
  other arithmetic  23.5 us (3%)
  starting transfers between devices  21.2 us (2%)
  between operations  21.1 us (2%)
  local copies, waits for them, and re-layouts  18.4 us (2%)
    psum x1, waiting for transfers between devices, on_device(): lax.psum((grad_down_part, grad_up_part), ('pair', 'seq', 'dp'))  265 us
    all_gather x1, waiting for transfers between devices, on_device(): lax.all_gather(image_rows_normed, 'seq', axis=0, tiled=True)  144 us
    all_gather x1, waiting for transfers between devices, on_device(): projection = lax.all_gather(image_output_weight, 'seq', axis=0, tiled=True)  107 us
    all_gather x1, waiting for transfers between devices, on_device(): lax.all_gather(txt_normed, 'seq', axis=0, tiled=True)  68.4 us
    all_gather x1, blocking collectives, on_device(): modulation = lax.all_gather(part_mod, 'seq', axis=1, tiled=True)[0]  38 us
    psum x1, blocking collectives, on_device(): err_ref, err_pol = lax.psum((terms[0][0], terms[1][0]), 'seq')  31.5 us
  transfers between devices with their start and end apart: 9, of which 9 were waited for; matrix products, arithmetic and copies ran while one was open for 7% of the time, Pallas kernels for 0%

commit v1 on v0

v1 whole, which is shorter than its diff:
```python
import functools
import math

import jax
import jax.numpy as jnp
from jax import lax
from jax.experimental import pallas as pl
from jax.experimental.pallas import tpu as pltpu
from jax.sharding import PartitionSpec as P

epsilon = 1e-06
half_beta = 20.0
horizon = 1000.0
F32 = jnp.float32
BF16 = jnp.bfloat16
VMEM_BYTES = 58 * 1024 * 1024


def sinusoid(step_value, width):
    half_width = width // 2
    freqs = jnp.exp(-math.log(10000.0) * jnp.arange(half_width, dtype=jnp.float32) / half_width)
    angle = step_value * freqs
    return jnp.concatenate([jnp.cos(angle), jnp.sin(angle)])


def mm(a, b):
    return lax.dot_general(a, b, (((1,), (0,)), ((), ())), preferred_element_type=F32)


def mm_nt(a, b):
    return lax.dot_general(a, b, (((1,), (1,)), ((), ())), preferred_element_type=F32)


def mm_tn(a, b):
    return lax.dot_general(a, b, (((0,), (0,)), ((), ())), preferred_element_type=F32)


def halves(a):
    top = a.astype(BF16)
    return top, (a - top.astype(F32)).astype(BF16)


def stacked(a):
    top, rest = halves(a)
    return jnp.concatenate([top, rest], 0)


def row_mean(a):
    return jnp.mean(a, -1, keepdims=True)


def rms_rows(rows):
    return lax.rsqrt(row_mean(rows * rows) + epsilon)


def remote(src, dst, send, recv, device):
    return pltpu.make_async_remote_copy(
        src_ref=src,
        dst_ref=dst,
        send_sem=send,
        recv_sem=recv,
        device_id=device,
        device_id_type=pl.DeviceIdType.MESH,
    )


def each(count, body):
    @pl.loop(0, count)
    def _(i):
        body(i)


def others(me, count, body):
    @pl.loop(1, count)
    def _(step):
        body(lax.rem(me + step, count))


def greet(axes):
    barrier = pltpu.get_barrier_semaphore()
    total = 0
    for axis, me, count in axes:
        others(
            me,
            count,
            lambda peer: pl.semaphore_signal(
                barrier,
                inc=1,
                device_id={axis: peer},
                device_id_type=pl.DeviceIdType.MESH,
            ),
        )
        total += count - 1
    return barrier, total


def at_rows(start, size):
    return pl.ds(pl.multiple_of(start, 16), size)


def at_lanes(start, size):
    return pl.ds(pl.multiple_of(start, 128), size)


def with_shift(scaled, shift):
    width = shift.shape[1]
    top, rest = halves(shift)
    which = lax.broadcasted_iota(jnp.int32, (16, width), 0)
    extra = jnp.where(
        which == 0,
        top.astype(F32),
        jnp.where(which == 1, rest.astype(F32), 0.0),
    )
    return jnp.concatenate([scaled, extra], 0).astype(BF16)


def front_kernel(
    seqs, dps, level, emb, lat, noi, txt, embed, wmod, wimg, wtxt, qg, kg, adown, aup, wo, lw,
    x, nz, mod, moddp, qp, kk, vext, pol, lhs, outf, rl, nn, ne, shl,
    noisy, text, oacc, q2, outb, modrow,
    mod_s, mod_r, noi_s, noi_r, txt_s, txt_r, nz_s, nz_r, dp_s, dp_r, kv_s, kv_r, x_s, x_r,
):
    me = lax.axis_index("seq")
    slot = lax.axis_index("pair")
    mine = lax.axis_index("dp")
    rows = lat.shape[0]
    images = rows * seqs
    width = embed.shape[1]
    half = txt.shape[0] // 2
    texts = half * seqs
    block = 4 * rows
    blocks = images // block
    part = wmod.shape[1]
    barrier, total = greet([("seq", me, seqs), ("dp", mine, dps), ("pair", slot, 2)])

    mod_part = mm(emb[...], wmod[...])[0:1]
    modrow[...] = mod_part
    lev = level[0, 0]
    noisy_mine = (
        (1.0 - lev) * lat[...].astype(F32) + lev * noi[...].astype(F32)
    ).astype(BF16)
    noisy[at_rows(me * rows, rows), :] = jnp.concatenate([noisy_mine, noisy_mine], 1)
    t = txt[at_rows(slot * half, half), :].astype(F32)
    t = t - row_mean(t)
    text[at_rows(me * half, half), :] = (t * lax.rsqrt(row_mean(t * t) + epsilon)).astype(BF16)
    pl.semaphore_wait(barrier, total)

    def mod_copy(owner, peer):
        return remote(
            modrow,
            mod.at[:, at_lanes(owner * part, part)],
            mod_s.at[peer],
            mod_r.at[owner],
            {"seq": peer},
        )

    def noisy_copy(owner, peer):
        where = noisy.at[at_rows(owner * rows, rows)]
        return remote(where, where, noi_s.at[peer], noi_r.at[owner], {"seq": peer})

    def text_copy(owner, peer):
        where = text.at[at_rows(owner * half, half)]
        return remote(where, where, txt_s.at[peer], txt_r.at[owner], {"seq": peer})

    def nz_copy(owner, peer):
        where = nz.at[at_rows(owner * 128, 128)]
        return remote(where, where, nz_s.at[peer], nz_r.at[owner], {"seq": peer})

    def dp_copy(owner, peer):
        return remote(
            mod.at[:, pl.ds(0, 2 * width)],
            moddp.at[owner],
            dp_s.at[peer],
            dp_r.at[owner],
            {"dp": peer},
        )

    def send_small(peer):
        mod_copy(me, peer).start()
        noisy_copy(me, peer).start()

    others(me, seqs, send_small)
    others(me, seqs, lambda peer: text_copy(me, peer).start())
    mod[:, at_lanes(me * part, part)] = mod_part

    emb_c = embed[...].astype(F32)
    emb_c = emb_c - row_mean(emb_c)
    e_top, e_rest = halves(emb_c)
    gram = stacked(mm_nt(e_top, e_top) + mm_nt(e_top, e_rest) + mm_nt(e_rest, e_top))
    wo_c = wo[...].astype(F32)
    wo_c = wo_c - row_mean(wo_c)
    zt = mm_nt(wo_c.astype(BF16), e_top)

    others(me, seqs, lambda peer: mod_copy(peer, peer).wait_recv())
    shift_img, scale_img, shift_txt, scale_txt, shift_out, scale_out = [
        mod[:, i * width : (i + 1) * width] for i in range(6)
    ]
    moddp[mine] = mod[:, 0 : 2 * width]
    others(mine, dps, lambda peer: dp_copy(mine, peer).start())
    ch = embed.shape[0]
    n_mine = mm((wo_c * (1.0 + scale_out)).astype(BF16), lw[...])
    nz[at_rows(me * 128, 128), :] = jnp.concatenate([n_mine, zt], 1).astype(BF16)
    others(me, seqs, lambda peer: nz_copy(me, peer).start())

    img_lhs = with_shift(emb_c * (1.0 + scale_img), shift_img)
    img_m = mm(img_lhs, wimg[...])
    img_m2 = stacked(img_m[0:ch])
    img_shift = img_m[ch : ch + 1] + img_m[ch + 1 : ch + 2]
    low_m = mm(img_lhs, adown[...])
    low_m2 = stacked(low_m[0:ch])
    low_shift = low_m[ch : ch + 1] + low_m[ch + 1 : ch + 2]
    out_m = mm(with_shift(emb_c * (1.0 + scale_out), shift_out), lw[...])
    out_m2 = stacked(out_m[0:ch])
    shl[...] = jnp.broadcast_to(out_m[ch : ch + 1] + out_m[ch + 1 : ch + 2], shl.shape)
    up = aup[:, at_lanes(me * 128, 128)]
    gain_q = qg[...]
    gain_k = kg[...]
    score_scale = math.log2(math.e) / math.sqrt(128.0)

    own = noisy[at_rows(me * rows, rows), :]
    ne[...] = mm(own, out_m2)
    own_nn = jnp.sum(mm(own, gram) * own[:, 0:ch].astype(F32), -1, keepdims=True)
    nn[...] = jnp.broadcast_to(own_nn, nn.shape)
    vext[:, 128:256] = jnp.ones((vext.shape[0], 128), BF16)

    others(me, seqs, lambda peer: noisy_copy(peer, peer).wait_recv())

    def project(i):
        here = at_rows(i * block, block)
        nb = noisy[here, :]
        nf = nb[:, 0:ch].astype(F32)
        var = jnp.sum(mm(nb, gram) * nf, -1, keepdims=True) * (1.0 / width)
        inv = lax.rsqrt(var + epsilon)
        qkv = mm(nb, img_m2) * inv + img_shift
        low = (mm(nb, low_m2) * inv + low_shift).astype(BF16)
        delta = mm(low, up).astype(BF16).astype(F32)
        q = qkv[:, 0:128]
        k = qkv[:, 128:256]
        q_pol = q + delta
        q2[here, :] = (q * rms_rows(q) * (gain_q * score_scale)).astype(BF16)
        qpol = (q_pol * rms_rows(q_pol) * (gain_q * score_scale)).astype(BF16)
        q2[at_rows(images + i * block, block), :] = qpol
        qp[here, :] = qpol
        pol[here, :] = q_pol
        kk[here, :] = (k * rms_rows(k) * gain_k).astype(BF16)
        vext[here, 0:128] = qkv[:, 256:384].astype(BF16)
        lhs[here, :] = jnp.concatenate([low, (nf * inv).astype(BF16)], 1)

    each(blocks, project)

    def attend(here, keys):
        s = mm_nt(q2[here, :], kk[keys, :])
        return mm(jnp.exp2(s).astype(BF16), vext[keys, :])

    def image_keys(i):
        here = at_rows(i * block, block)
        oacc[here, :] = attend(here, pl.ds(0, images))

    each(2 * blocks, image_keys)

    others(me, seqs, lambda peer: text_copy(peer, peer).wait_recv())
    text_n = (text[...].astype(F32) * (1.0 + scale_txt) + shift_txt).astype(BF16)
    kv = mm(text_n, wtxt[...])
    k = kv[:, 0:128]
    my_keys = at_rows(images + slot * texts, texts)
    kk[my_keys, :] = (k * rms_rows(k) * gain_k).astype(BF16)
    vext[my_keys, 0:128] = kv[:, 128:256].astype(BF16)
    other = 1 - slot

    def kv_copies(owner):
        keys = at_rows(images + owner * texts, texts)
        v = vext.at[keys, pl.ds(0, 128)]
        return (
            remote(kk.at[keys], kk.at[keys], kv_s.at[0], kv_r.at[0], {"pair": other}),
            remote(v, v, kv_s.at[1], kv_r.at[1], {"pair": other}),
        )

    for copy in kv_copies(slot):
        copy.start()
    for copy in kv_copies(other):
        copy.wait_recv()

    def out_copy(kind, owner, peer):
        return remote(
            outb.at[at_rows(kind * images + peer * rows, rows)],
            x.at[at_rows(kind * rows, rows), at_lanes(owner * 128, 128)],
            x_s.at[kind, peer],
            x_r.at[kind, owner],
            {"seq": peer},
        )

    def text_keys(i):
        kind = lax.div(i, blocks)
        b = lax.rem(i + lax.div(me, 4), blocks)
        here = at_rows(kind * images + b * block, block)
        o = oacc[here, :] + attend(here, pl.ds(images, 2 * texts))
        inv = 1.0 / o[:, 128:256]
        out = o[:, 0:128] * inv
        outb[here, :] = out.astype(BF16)

        @pl.when(kind == 1)
        def _():
            outf[at_rows(b * block, block), :] = out
            rl[at_rows(b * block, block), :] = inv

        for j in range(4):
            peer = b * 4 + j

            @pl.when(peer != me)
            def _():
                out_copy(kind, me, peer).start()

            @pl.when(peer == me)
            def _():
                x[at_rows(kind * rows, rows), at_lanes(me * 128, 128)] = outb[
                    at_rows(kind * images + me * rows, rows), :
                ]

    each(2 * blocks, text_keys)

    def finish(peer):
        mod_copy(me, peer).wait_send()
        noisy_copy(me, peer).wait_send()
        text_copy(me, peer).wait_send()
        nz_copy(me, peer).wait_send()
        nz_copy(peer, peer).wait_recv()
        for kind in range(2):
            out_copy(kind, me, peer).wait_send()
            out_copy(kind, peer, peer).wait_recv()

    others(me, seqs, finish)

    def finish_dp(peer):
        dp_copy(mine, peer).wait_send()
        dp_copy(peer, peer).wait_recv()

    others(mine, dps, finish_dp)
    for copy in kv_copies(slot):
        copy.wait_send()


def middle_kernel(
    seqs, dps, model, sign, x, nz, kb, lat, noi, nown, nn, ne, shl, qp, kk, vext, pol, lhs, outf, rl, qg, aup,
    ua, value,
    km, ghs, gh, gapbuf, acc, csum,
    k_sem, g_s, g_r, e_s, e_r,
):
    me = lax.axis_index("seq")
    slot = lax.axis_index("pair")
    rows = lat.shape[0]
    ch = lat.shape[1]
    images = rows * seqs
    width = 128 * seqs
    model_width = float(model)
    count = kb.shape[0]
    barrier, total = greet([("seq", me, seqs), ("pair", slot, 2)])
    other = 1 - slot

    others(
        me,
        seqs,
        lambda peer: pl.semaphore_signal(
            barrier,
            inc=1,
            device_id={"seq": peer, "pair": other},
            device_id_type=pl.DeviceIdType.MESH,
        ),
    )

    def k_copy(i):
        h = lax.rem(i, seqs)
        j = lax.rem(h + lax.div(i, seqs), seqs)
        return pltpu.make_async_copy(
            kb.at[i], km.at[at_rows(h * 128, 128), at_lanes(j * 128, 128)], k_sem.at[0]
        )

    each(count, lambda i: k_copy(i).start())
    each(count, lambda i: k_copy(i).wait())
    xv = x[...]
    y = mm(xv, km[...])
    xn = mm(xv, nz[...])
    own = nown[:, 0:ch].astype(F32)
    noise2 = jnp.concatenate([own, own], 0)
    nn2 = jnp.concatenate([nn[:, 0:1], nn[:, 0:1]], 0)
    ne2 = jnp.concatenate([ne[...], ne[...]], 0)
    quad = (
        nn2
        + 2.0 * jnp.sum(noise2 * xn[:, ch : 2 * ch], -1, keepdims=True)
        + jnp.sum(xv.astype(F32) * y, -1, keepdims=True)
    )
    inv = lax.rsqrt(quad * (1.0 / model_width) + epsilon)
    proj = inv * (xn[:, 0:ch] + ne2)
    target = noi[...].astype(F32) - lat[...].astype(F32)
    diff = jnp.concatenate([target, target], 0) - (proj + shl[0:1, :])
    squares = diff * diff
    gap = (jnp.sum(squares[rows:]) - jnp.sum(squares[:rows])) * (1.0 / (images * ch))
    gapbuf[slot * seqs + me] = jnp.full((8, 128), gap, F32)

    d = diff[rows:]
    inv_p = inv[rows:]
    m = jnp.sum(d * proj[rows:], -1, keepdims=True) * (1.0 / model_width) * inv_p
    left = jnp.concatenate([d, -m * own], 1).astype(BF16)
    ghs[...] = (inv_p * (mm_nt(left, nz[...]) - m * y[rows:])).astype(BF16)

    pl.semaphore_wait(barrier, total + seqs - 1)

    def g_copy(owner, peer):
        return remote(
            ghs.at[:, at_lanes(peer * 128, 128)],
            gh.at[at_rows(owner * rows, rows)],
            g_s.at[peer],
            g_r.at[owner],
            {"seq": peer},
        )

    def gap_copy(to_slot, from_slot, owner, peer):
        return remote(
            gapbuf.at[slot * seqs + me],
            gapbuf.at[from_slot * seqs + owner],
            e_s.at[to_slot * seqs + peer],
            e_r.at[from_slot * seqs + owner],
            {"seq": peer, "pair": to_slot},
        )

    others(me, seqs, lambda peer: g_copy(me, peer).start())

    def send_gap(peer):
        gap_copy(slot, slot, me, peer).start()
        gap_copy(other, slot, me, peer).start()

    others(me, seqs, send_gap)
    gap_copy(other, slot, me, me).start()
    gh[at_rows(me * rows, rows), :] = ghs[:, at_lanes(me * 128, 128)]
    acc[...] = jnp.zeros_like(acc)
    csum[...] = jnp.zeros_like(csum)
    others(me, seqs, lambda peer: g_copy(peer, peer).wait_recv())
    block = 4 * rows
    gain = qg[...]
    keys = kk[...]
    vals = vext[:, 0:128]

    def back(i):
        here = at_rows(i * block, block)
        g = gh[here, :]
        p = jnp.exp2(mm_nt(qp[here, :], keys))
        gp = mm_nt(g, vals)
        dsum = jnp.sum(g.astype(F32) * outf[here, :], -1, keepdims=True)
        gs = (p * (gp - dsum)).astype(BF16)
        gq = mm(gs, keys) * (rl[here, :] * (1.0 / math.sqrt(128.0)))
        u = pol[here, :]
        r = rms_rows(u)
        w = gq * gain
        gd = (r * w - u * (r * r * r) * row_mean(u * w)).astype(BF16)
        acc[...] += mm_tn(lhs[here, :], gd)
        csum[...] += jnp.broadcast_to(
            jnp.sum(gd.astype(F32), 0, keepdims=True), csum.shape
        )

    each(images // block, back)

    def wait_gap(peer):
        gap_copy(slot, slot, peer, peer).wait_recv()
        gap_copy(slot, other, peer, peer).wait_recv()
        gap_copy(slot, slot, me, peer).wait_send()
        gap_copy(other, slot, me, peer).wait_send()
        g_copy(me, peer).wait_send()

    others(me, seqs, wait_gap)
    gap_copy(slot, other, me, me).wait_recv()
    gap_copy(other, slot, me, me).wait_send()
    own_gap = jnp.sum(gapbuf[pl.ds(slot * seqs, seqs)], 0)
    other_gap = jnp.sum(gapbuf[pl.ds(other * seqs, seqs)], 0)
    sgn = sign[0, 0]
    z = half_beta * sgn * (own_gap - other_gap)
    value[...] = jnp.maximum(z, 0.0) + jnp.log1p(jnp.exp(-jnp.abs(z)))
    weight = half_beta / dps / (1.0 + jnp.exp(-z))
    factor = (sgn * weight * (-2.0 / (images * ch)))[0:1, :]
    up = aup[:, at_lanes(me * 128, 128)]
    rank = up.shape[0]
    ua[0:rank, :] = acc[0:rank, :] * factor
    a_top, a_rest = halves(jnp.concatenate([acc[rank : rank + ch, :], csum[...]], 0))
    tail = mm_nt(a_top, up) + mm_nt(a_rest, up)
    ua[rank:, :] = jnp.concatenate([tail, tail], 1) * factor


def last_kernel(
    seqs, dps, ua, embed, moddp,
    down, upg,
    ubuf, abuf, a2, usum, asum, left, right,
    u_s, u_r, a_s, a_r, v_s, v_r, b_s, b_r,
):
    me = lax.axis_index("seq")
    slot = lax.axis_index("pair")
    mine = lax.axis_index("dp")
    width = embed.shape[1]
    ch = embed.shape[0]
    rank = upg.shape[0]
    tail = ua.shape[0] - rank
    reps = 2 * dps
    rep = slot * dps + mine
    barrier, total = greet([("seq", me, seqs)])

    def to(r):
        return {"pair": lax.div(r, dps), "dp": lax.rem(r, dps)}

    others(
        rep,
        reps,
        lambda peer: pl.semaphore_signal(
            barrier, inc=1, device_id=to(peer), device_id_type=pl.DeviceIdType.MESH
        ),
    )
    pl.semaphore_wait(barrier, total + reps - 1)

    def u_copy(owner, peer):
        return remote(
            ua.at[pl.ds(0, rank)], ubuf.at[owner], u_s.at[peer], u_r.at[owner], to(peer)
        )

    def a_copy(owner, peer):
        return remote(
            ua.at[pl.ds(rank, tail)], abuf.at[owner], a_s.at[peer], a_r.at[owner], {"seq": peer}
        )

    def v_copy(owner, peer):
        return remote(
            usum,
            upg.at[:, at_lanes(owner * 128, 128)],
            v_s.at[peer],
            v_r.at[owner],
            {"seq": peer},
        )

    def b_copy(owner, peer):
        return remote(asum, a2.at[owner], b_s.at[peer], b_r.at[owner], to(peer))

    others(rep, reps, lambda peer: u_copy(rep, peer).start())
    others(me, seqs, lambda peer: a_copy(me, peer).start())
    ubuf[rep] = ua[0:rank, :]
    abuf[me] = ua[rank:, :]
    emb_c = embed[...].astype(F32)
    emb_c = emb_c - row_mean(emb_c)
    first = lax.broadcasted_iota(jnp.int32, (8, width), 0) == 0
    for p in range(dps):
        shift = moddp[p, :, 0:width]
        scale = moddp[p, :, width:]
        scaled = emb_c * (1.0 + scale)
        extra = jnp.where(first, shift, 0.0)
        left[p * tail : (p + 1) * tail, :] = jnp.concatenate([scaled, extra], 0)
    others(rep, reps, lambda peer: u_copy(peer, peer).wait_recv())
    sums = jnp.sum(ubuf[...], 0)
    usum[...] = sums
    upg[:, at_lanes(me * 128, 128)] = sums
    others(me, seqs, lambda peer: v_copy(me, peer).start())
    others(me, seqs, lambda peer: a_copy(peer, peer).wait_recv())
    sums = jnp.sum(abuf[...], 0)
    asum[...] = sums
    a2[rep] = sums
    others(rep, reps, lambda peer: b_copy(rep, peer).start())
    others(rep, reps, lambda peer: b_copy(peer, peer).wait_recv())
    for p in range(dps):
        right[p * tail : (p + 1) * tail, :] = a2[p] + a2[dps + p]
    got = mm_tn(right[...].astype(BF16), left[...].astype(BF16))
    down[...] = got[0:ch, :].T

    def finish(peer):
        a_copy(me, peer).wait_send()
        v_copy(me, peer).wait_send()
        v_copy(peer, peer).wait_recv()

    others(me, seqs, finish)

    def finish_reps(peer):
        u_copy(rep, peer).wait_send()
        b_copy(rep, peer).wait_send()

    others(rep, reps, finish_reps)


def shape(dims, kind):
    return jax.ShapeDtypeStruct(dims, kind)


def call(kernel, ident, specs, outs, scratch, cost, *operands):
    return pl.pallas_call(
        kernel,
        out_shape=outs,
        in_specs=[pl.BlockSpec(memory_space=s) for s in specs],
        out_specs=[pl.BlockSpec(memory_space=pltpu.VMEM)] * len(outs),
        scratch_shapes=scratch,
        compiler_params=pltpu.CompilerParams(
            collective_id=ident, has_side_effects=True, vmem_limit_bytes=VMEM_BYTES
        ),
        cost_estimate=pl.CostEstimate(flops=cost, bytes_accessed=16 << 20, transcendentals=0),
    )(*operands)


def on_device(
    latents,
    noise,
    pair_timestep_index,
    preferred_image_slot,
    prompt_token_states,
    image_embed_weight,
    timestep_modulation_weight,
    image_query_key_value,
    text_key_value,
    query_norm_gain,
    key_norm_gain,
    adapter_down_weight,
    adapter_up_weight,
    image_output_weight,
    latent_out_weight,
):
    seqs = lax.axis_size("seq")
    dps = lax.axis_size("dp")
    slot = lax.axis_index("pair")
    rows, ch = latents.shape[2:]
    images = rows * seqs
    width = image_embed_weight.shape[1]
    texts = prompt_token_states.shape[1] * seqs
    keys = images + texts
    rank = adapter_down_weight.shape[1]
    step_value = pair_timestep_index[0].astype(jnp.float32)
    level = ((step_value + 1.0) / horizon).reshape(1, 1)
    emb = jnp.broadcast_to(
        sinusoid(step_value, timestep_modulation_weight.shape[0]).astype(BF16)[None],
        (16, timestep_modulation_weight.shape[0]),
    )
    lat = latents[0, 0]
    noi = noise[0]

    everyone = ("pair", "seq", "dp")
    moves = []
    for s in range(2):
        for h in range(seqs):
            for p in range(dps):
                source = (h + s * dps + p) % seqs
                moves.append(((s * seqs + source) * dps + p, (s * seqs + h) * dps + p))
    wo_c = image_output_weight.astype(F32)
    wo_c = (wo_c - jnp.mean(wo_c, -1, keepdims=True)).astype(BF16)
    wo_other = lax.ppermute(wo_c, everyone, moves)
    kb = lax.all_gather(mm_nt(wo_c, wo_other).astype(BF16), "seq")
    kb = lax.all_gather(kb, ("pair", "dp")).reshape(2, dps, seqs, 128, 128)
    kb = kb.reshape(-1, 128, 128)

    V, S, A = pltpu.VMEM, pltpu.SMEM, pl.ANY
    DMA = pltpu.SemaphoreType.DMA
    outs = [
        shape((2 * rows, 128 * seqs), BF16),
        shape((128 * seqs, 128), BF16),
        shape((1, 6 * width), F32),
        shape((dps, 1, 2 * width), F32),
        shape((images, 128), BF16),
        shape((keys, 128), BF16),
        shape((keys, 256), BF16),
        shape((images, 128), F32),
        shape((images, 128), BF16),
        shape((images, 128), F32),
        shape((images, 128), F32),
        shape((rows, 128), F32),
        shape((rows, ch), F32),
        shape((8, ch), F32),
    ]
    scratch = [
        V((images, 128), BF16),
        V((texts // 2, width), BF16),
        V((2 * images, 256), F32),
        V((2 * images, 128), BF16),
        V((2 * images, 128), BF16),
        V((1, timestep_modulation_weight.shape[1]), F32),
    ]
    scratch += [DMA((seqs,))] * 8 + [DMA((dps,))] * 2 + [DMA((2,))] * 2 + [DMA((2, seqs))] * 2
    front = call(
        functools.partial(front_kernel, seqs, dps),
        0,
        [S] + [V] * 14,
        outs,
        scratch,
        20 * 10**9,
        level,
        emb,
        lat,
        noi,
        prompt_token_states[0],
        image_embed_weight,
        timestep_modulation_weight,
        image_query_key_value.reshape(width, -1),
        text_key_value.reshape(width, -1),
        query_norm_gain.reshape(1, -1),
        key_norm_gain.reshape(1, -1),
        adapter_down_weight,
        adapter_up_weight,
        image_output_weight,
        latent_out_weight,
    )
    x, nz, mod, moddp, qp, kk, vext, pol, lhs, outf, rl, nn, ne, shl = front
    del mod
    nown = ((1.0 - level) * lat.astype(F32) + level * noi.astype(F32)).astype(BF16)
    sign = jnp.where(preferred_image_slot[0] == slot, 1.0, -1.0).astype(F32).reshape(1, 1)
    tail = ch + 8
    scratch = [
        V((128 * seqs, 128 * seqs), BF16),
        V((rows, 128 * seqs), BF16),
        V((images, 128), BF16),
        V((2 * seqs, 8, 128), F32),
        V((rank + ch, 128), F32),
        V((8, 128), F32),
        DMA((1,)),
        DMA((seqs,)),
        DMA((seqs,)),
        DMA((2 * seqs,)),
        DMA((2 * seqs,)),
    ]
    ua, value = call(
        functools.partial(middle_kernel, seqs, dps, width),
        1,
        [S, V, V, A] + [V] * 15,
        [shape((rank + tail, 128), F32), shape((8, 128), F32)],
        scratch,
        10 * 10**9,
        sign,
        x,
        nz,
        kb,
        lat,
        noi,
        nown,
        nn,
        ne,
        shl,
        qp,
        kk,
        vext,
        pol,
        lhs,
        outf,
        rl,
        query_norm_gain.reshape(1, -1),
        adapter_up_weight,
    )
    reps = 2 * dps
    scratch = [
        V((reps, rank, 128), F32),
        V((seqs, tail, 128), F32),
        V((reps, tail, 128), F32),
        V((rank, 128), F32),
        V((tail, 128), F32),
        V((dps * tail, width), F32),
        V((dps * tail, 128), F32),
    ]
    scratch += [DMA((reps,))] * 2 + [DMA((seqs,))] * 4 + [DMA((reps,))] * 2
    down, upg = call(
        functools.partial(last_kernel, seqs, dps),
        2,
        [V] * 3,
        [shape((width, rank), F32), shape((rank, 128 * seqs), F32)],
        scratch,
        10**9,
        ua,
        image_embed_weight,
        moddp,
    )
    return (down, upg, value[0, 0:1])


def solution(mesh):
    return jax.shard_map(
        on_device,
        mesh=mesh,
        in_specs=(
            P("dp", "pair", "seq", None),
            P("dp", "seq", None),
            P("dp"),
            P("dp"),
            P("dp", "seq", None),
            P(),
            P(None, "seq"),
            P(None, "seq", None),
            P(None, "seq", None),
            P(),
            P(),
            P(),
            P(),
            P("seq", None),
            P(),
        ),
        out_specs=(P(), P(), P("dp")),
        check_vma=False,
    )
```

time: 873 us -> 283 us (0.32)
  waiting for transfers between devices: 629 us -> 9.65 us
  Pallas kernels: 0 us -> 195 us
  matrix products: 73.2 us -> 0.37 us
  blocking collectives: 84 us -> 39.7 us
  other arithmetic: 23.5 us -> 3.35 us
  local copies, waits for them, and re-layouts: 18.4 us -> 8 us
  starting transfers between devices: 21.2 us -> 11.1 us
    all_gather x3 -> x1, waiting for transfers between devices: 319 us -> 0.02 us  [on_device(): kb = lax.all_gather(kb, ('pair', 'dp')).reshape(2, dps, seqs, 128, 128)]
    psum x1 -> x0, waiting for transfers between devices: 265 us -> none  [on_device(): lax.psum((grad_down_part, grad_up_part), ('pair', 'seq', 'dp'))]
    pallas_call x0 -> x3, Pallas kernels: none -> 195 us  [call(): pl.pallas_call(kernel, out_shape=outs, in_specs=[pl.BlockSpec(memory_spac...]
    dot_general x35 -> x1, matrix products: 73.2 us -> 0.37 us  [mm_nt(): lax.dot_general(a, b, (((1,), (1,)), ((), ())), preferred_element_type=F32)]
    all_to_all x4 -> x0, waiting for transfers between devices: 44.2 us -> none  [the longest x1 11.9 us: on_device(): lax.all_to_all(both_out[images:], 'seq', split_axis=0, concat_axis=1, til...]
    psum x1 -> x0, blocking collectives: 31.5 us -> none  [on_device(): err_ref, err_pol = lax.psum((terms[0][0], terms[1][0]), 'seq')]
    all_to_all x4 -> x0, starting transfers between devices: 18.9 us -> none  [the longest x1 6.43 us: on_device(): lax.all_to_all(both_out[images:], 'seq', split_axis=0, concat_axis=1, til...]
    all_to_all x1 -> x0, blocking collectives: 14.5 us -> none  [on_device(): lax.all_to_all(grad_query_change, 'seq', split_axis=0, concat_axis=1, til...]
  transfers between devices with their start and end apart: 9 -> 2, of which waited for: 9 -> 1; matrix products, arithmetic and copies ran while one was open for 7% -> 1% of each run, Pallas kernels for 0% -> 43%
where the time goes in v1:
time: 283 us; the launch traced here: 282 us
  Pallas kernels  195 us (69%)
  blocking collectives  39.7 us (14%)
  between operations  15.5 us (5%)
  starting transfers between devices  11.1 us (4%)
  waiting for transfers between devices  9.65 us (3%)
  local copies, waits for them, and re-layouts  8 us (3%)
  other arithmetic  3.35 us (1%)
    pallas_call x3, Pallas kernels, call(): pl.pallas_call(kernel, out_shape=outs, in_specs=[pl.BlockSpec(memory_spac...  195 us
    all_gather x1, blocking collectives, on_device(): kb = lax.all_gather(mm_nt(wo_c, wo_other).astype(BF16), 'seq')  39.7 us
    ppermute x1, starting transfers between devices, on_device(): wo_other = lax.ppermute(wo_c, everyone, moves)  11.1 us
    ppermute x1, waiting for transfers between devices, on_device(): wo_other = lax.ppermute(wo_c, everyone, moves)  9.61 us
    unnamed x20, local copies, waits for them, and re-layouts  6.22 us
  transfers between devices with their start and end apart: 2, of which 1 were waited for; matrix products, arithmetic and copies ran while one was open for 1% of the time, Pallas kernels for 43%

profile of v1, /device:TPU:1, one launch (start us, length us, event | category | flops | bytes accessed | tf_op | source)
XLA Modules:
  0.0 282.4 jit_solution(12152267417534627895)
XLA Ops:
  7.2 0.0 all-gather.4.cloned.1.call-start
  7.2 1.3 convert_reduce_fusion
  8.5 1.3 fusion
  9.9 0.0 copy-start.5
  9.9 0.0 copy-start.6
  9.9 0.0 copy-start.1
  9.9 11.1 %collective-permute-start = (bf16[128,3072]{1,0:T(8,128)(2,1)S(1)}, bf16[128,3072]{1,0:T(8,128)(2,1)S(1)}, u32[]{:S(2)}, u32[]{:S(2)}) collective-permute-start(bf16[128,3072]{1,0:T(8,128)(2,1)S(1)} %fusion), channel_id=1, source_target_pairs={{0,0},{9,1},{18,2},{27,3},{36,4},{45,5},{54,6},{63,7},{8,8},{17,9}... | collective-permute-start | bytes 2359304 | tf_op jit(solution)/shard_map/ppermute | solution.py:642
  21.0 9.6 %collective-permute-done = bf16[128,3072]{1,0:T(8,128)(2,1)S(1)} collective-permute-done((bf16[128,3072]{1,0:T(8,128)(2,1)S(1)}, bf16[128,3072]{1,0:T(8,128)(2,1)S(1)}, u32[]{:S(2)}, u32[]{:S(2)}) %collective-permute-start) | collective-permute-done | bytes 786464 | tf_op jit(solution)/shard_map/ppermute | solution.py:642
  30.6 0.4 convolution_convert_fusion
  31.0 0.0 copy-start.2
  31.0 39.7 %all-gather = bf16[2048,128]{1,0:T(8,128)(2,1)} all-gather(bf16[128,128]{1,0:T(8,128)(2,1)S(1)} %convolution_convert_fusion), channel_id=2, replica_groups=mesh['pair'=2,'seq'=16,'dp'=8] {'seq'}, dimensions={0}, use_global_device_ids=true | all-gather | bytes 557056 | tf_op jit(solution)/shard_map/all_gather | solution.py:643
  70.7 0.0 all-gather.4.cloned.1.call-update
  72.1 0.0 copy-done.5
  72.1 0.1 copy.23
  72.2 0.0 copy-done.6
  72.2 0.0 copy-start.3
  72.2 0.1 copy.24
  72.3 0.0 copy-done.1
  72.3 0.0 copy-start.4
  72.3 1.2 copy.25.adown
  73.5 0.0 copy-done.2
  73.5 1.2 copy.26.lw
  74.8 0.6 add_convert_fusion.nown
  75.4 0.6 broadcast_in_dim.2.emb
  76.0 0.0 copy-done.3
  76.0 0.0 copy-done.4
  76.0 122.4 %shard_map.166 = (bf16[192,2048]{1,0:T(8,128)(2,1)}, bf16[2048,128]{1,0:T(8,128)(2,1)}, f32[1,18432]{1,0:T(1,128)}, f32[8,1,6144]{2,1,0:T(1,128)}, bf16[1536,128...) custom-call(f32[1,1]{1,0:T(1,128)} %bitcast.3.level, ...), custom_call_target="tpu_custom_call" | custom-call | flops 20000000000 | bytes 16777216 | tf_op jit(solution)/shard_map/pallas_call | solution.py:585
  198.4 0.0 all-gather.4.cloned.1.call-done.kb
  198.4 32.4 %shard_map.167 = (f32[136,128]{1,0:T(8,128)}, f32[8,128]{1,0:T(8,128)}) custom-call(f32[1,1]{1,0:T(1,128)} %bitcast.1.sign, bf16[192,2048]{1,0:T(8,128)(2,1)} %get-tuple-element.20.x, bf16[2048,128]{1,0:T(8,128)(2,1)} %get-tuple-element.21.nz, bf16[256,128,128]{2,1,0:T(8,128)(2,1)} %all-gather.4.cloned.1.call-done.kb, bf16[96,64]{1,0:T(8,128)(2,1)} %bitcast.21, ...), custom_call_target="tpu_custom_call" | custom-call | flops 10000000000 | bytes 16777216 | tf_op jit(solution)/shard_map/pallas_call | solution.py:585
  230.8 39.9 %shard_map.168 = (f32[3072,64]{1,0:T(8,128)}, f32[64,2048]{1,0:T(8,128)}) custom-call(f32[136,128]{1,0:T(8,128)} %get-tuple-element.32.ua, bf16[64,3072]{1,0:T(8,128)(2,1)} %embed.3, f32[8,1,6144]{2,1,0:T(1,128)} %get-tuple-element.33.moddp), custom_call_target="tpu_custom_call" | custom-call | flops 1000000000 | bytes 16777216 | tf_op jit(solution)/shard_map/pallas_call | solution.py:585
  270.8 0.0 copy-start
  270.8 2.8 copy.27
  273.6 1.2 slice.3
  274.8 0.0 copy-done
  274.8 0.8 copy.31
  (3 shorter events, 0.1 us)
Async XLA Ops:
  7.2 191.3 %all-gather.4.cloned.1.call-start = ((), (), s32[]{:S(2)}) async-start(), calls=%async_computation | async-start | bytes 8912896 | tf_op jit(solution)/shard_map/all_gather | solution.py:644
  9.9 62.2 %copy-start.5 = (bf16[1,1,96,64]{2,3,1,0:T(8,128)(2,1)S(1)}, bf16[1,1,96,64]{2,3,1,0:T(8,128)(2,1)}, u32[]{:S(2)}) copy-start(bf16[1,1,96,64]{2,3,1,0:T(8,128)(2,1)} %param.15) | copy-start | bytes 36868
  9.9 62.3 %copy-start.6 = (bf16[1,96,64]{1,2,0:T(8,128)(2,1)S(1)}, bf16[1,96,64]{1,2,0:T(8,128)(2,1)}, u32[]{:S(2)}) copy-start(bf16[1,96,64]{1,2,0:T(8,128)(2,1)} %param.16) | copy-start | bytes 36868
  9.9 62.4 %copy-start.1 = (bf16[3072,64]{0,1:T(8,128)(2,1)S(1)}, bf16[3072,64]{0,1:T(8,128)(2,1)}, u32[]{:S(2)}) copy-start(bf16[3072,64]{0,1:T(8,128)(2,1)} %param.26) | copy-start | bytes 1179652
  9.9 20.7 %collective-permute-start = (bf16[128,3072]{1,0:T(8,128)(2,1)S(1)}, bf16[128,3072]{1,0:T(8,128)(2,1)S(1)}, u32[]{:S(2)}, u32[]{:S(2)}) collective-permute-start(bf16[128,3072]{1,0:T(8,128)(2,1)S(1)} %fusion), channel_id=1, source_target_pairs={{0,0},{9,1},{18,2},{27,3},{36,4},{45,5},{54,6},{63,7},{8,8},{17,9}... | collective-permute-start | bytes 2359304 | tf_op jit(solution)/shard_map/ppermute | solution.py:642
  31.0 42.5 %copy-start.2 = (bf16[3072,64]{0,1:T(8,128)(2,1)S(1)}, bf16[3072,64]{0,1:T(8,128)(2,1)}, u32[]{:S(2)}) copy-start(bf16[3072,64]{0,1:T(8,128)(2,1)} %param.29) | copy-start | bytes 1179652
  72.2 3.8 %copy-start.3 = (bf16[1,1,96,64]{3,2,1,0:T(8,128)(2,1)}, bf16[1,1,96,64]{3,2,1,0:T(8,128)(2,1)S(1)}, u32[]{:S(2)}) copy-start(bf16[1,1,96,64]{3,2,1,0:T(8,128)(2,1)S(1)} %copy.23) | copy-start | bytes 36868
  72.3 3.7 %copy-start.4 = (bf16[1,96,64]{2,1,0:T(8,128)(2,1)}, bf16[1,96,64]{2,1,0:T(8,128)(2,1)S(1)}, u32[]{:S(2)}) copy-start(bf16[1,96,64]{2,1,0:T(8,128)(2,1)S(1)} %copy.24) | copy-start | bytes 36868
  270.8 4.0 %copy-start = (f32[64,2048]{1,0:T(8,128)S(1)}, f32[64,2048]{1,0:T(8,128)}, u32[]{:S(2)}) copy-start(f32[64,2048]{1,0:T(8,128)} %get-tuple-element.49) | copy-start | bytes 1572868
Sparse Core Ops, SparseCore 0:
  70.9 125.4 all-gather.3

commit v2 on v1

v2 whole, which is shorter than its diff:
```python
import functools
import math

import jax
import jax.numpy as jnp
from jax import lax
from jax.experimental import pallas as pl
from jax.experimental.pallas import tpu as pltpu
from jax.sharding import PartitionSpec as P

epsilon = 1e-06
half_beta = 20.0
horizon = 1000.0
F32 = jnp.float32
BF16 = jnp.bfloat16
VMEM_BYTES = 58 * 1024 * 1024


def sinusoid(step_value, width):
    half_width = width // 2
    freqs = jnp.exp(-math.log(10000.0) * jnp.arange(half_width, dtype=jnp.float32) / half_width)
    angle = step_value * freqs
    return jnp.concatenate([jnp.cos(angle), jnp.sin(angle)])


def mm(a, b):
    return lax.dot_general(a, b, (((1,), (0,)), ((), ())), preferred_element_type=F32)


def mm_nt(a, b):
    return lax.dot_general(a, b, (((1,), (1,)), ((), ())), preferred_element_type=F32)


def mm_tn(a, b):
    return lax.dot_general(a, b, (((0,), (0,)), ((), ())), preferred_element_type=F32)


def halves(a):
    top = a.astype(BF16)
    return top, (a - top.astype(F32)).astype(BF16)


def stacked(a):
    top, rest = halves(a)
    return jnp.concatenate([top, rest], 0)


def row_mean(a):
    return jnp.mean(a, -1, keepdims=True)


def rms_rows(rows):
    return lax.rsqrt(row_mean(rows * rows) + epsilon)


def remote(src, dst, send, recv, device):
    return pltpu.make_async_remote_copy(
        src_ref=src,
        dst_ref=dst,
        send_sem=send,
        recv_sem=recv,
        device_id=device,
        device_id_type=pl.DeviceIdType.MESH,
    )


def each(count, body):
    @pl.loop(0, count)
    def _(i):
        body(i)


def others(me, count, body):
    @pl.loop(1, count)
    def _(step):
        body(lax.rem(me + step, count))


def greet(axes):
    barrier = pltpu.get_barrier_semaphore()
    total = 0
    for axis, me, count in axes:
        others(
            me,
            count,
            lambda peer: pl.semaphore_signal(
                barrier,
                inc=1,
                device_id={axis: peer},
                device_id_type=pl.DeviceIdType.MESH,
            ),
        )
        total += count - 1
    return barrier, total


def at_rows(start, size):
    return pl.ds(pl.multiple_of(start, 16), size)


def at_lanes(start, size):
    return pl.ds(pl.multiple_of(start, 128), size)


def with_shift(scaled, shift):
    width = shift.shape[1]
    top, rest = halves(shift)
    which = lax.broadcasted_iota(jnp.int32, (16, width), 0)
    extra = jnp.where(
        which == 0,
        top.astype(F32),
        jnp.where(which == 1, rest.astype(F32), 0.0),
    )
    return jnp.concatenate([scaled, extra], 0).astype(BF16)


def main_kernel(
    seqs, dps, level, sign, emb, lat, noi, txt, embed, wmod, wimg, wtxt, qg, kg, adown_t, aup, wo, lw_t,
    ua, value, moddp,
    mod, noisy, text, oacc, q2, outb, modrow, x, wall, kk, vext, pol, lhs, outf, rl,
    mixed, gmix, gh, ghs, gapbuf, acc, csum,
    mod_s, mod_r, noi_s, noi_r, txt_s, txt_r, dp_s, dp_r, kv_s, kv_r, x_s, x_r,
    g_s, g_r, e_s, e_r, wz_s, wz_r, wx_s, wx_r, wy_s, wy_r, wc_s, wc_r,
):
    me = lax.axis_index("seq")
    slot = lax.axis_index("pair")
    mine = lax.axis_index("dp")
    other = 1 - slot
    rows, ch = lat.shape
    images = rows * seqs
    width = embed.shape[1]
    span = width // 2
    strip = 128 // dps
    ring = dps // 2
    half = txt.shape[0] // 2
    texts = half * seqs
    block = 4 * rows
    blocks = images // block
    part = wmod.shape[1]
    barrier, total = greet([("seq", me, seqs), ("dp", mine, dps)])
    total += seqs

    def greet_other(peer):
        pl.semaphore_signal(
            barrier,
            inc=1,
            device_id={"seq": peer, "pair": other},
            device_id_type=pl.DeviceIdType.MESH,
        )

    each(seqs, greet_other)

    mod_part = mm(emb[...], wmod[...])[0:1]
    modrow[...] = mod_part
    lev = level[0, 0]
    noisy_mine = (
        (1.0 - lev) * lat[...].astype(F32) + lev * noi[...].astype(F32)
    ).astype(BF16)
    noisy[at_rows(me * rows, rows), :] = jnp.concatenate([noisy_mine, noisy_mine], 1)
    mine_rows, mine_cols = at_rows(mine * strip, strip), at_lanes(slot * span, span)
    wall[me, mine_rows, mine_cols] = wo[mine_rows, mine_cols]
    t = txt[at_rows(slot * half, half), :].astype(F32)
    t = t - row_mean(t)
    text[at_rows(me * half, half), :] = (t * lax.rsqrt(row_mean(t * t) + epsilon)).astype(BF16)
    pl.semaphore_wait(barrier, total)

    def mod_copy(owner, peer):
        return remote(
            modrow,
            mod.at[:, at_lanes(owner * part, part)],
            mod_s.at[peer],
            mod_r.at[owner],
            {"seq": peer},
        )

    def noisy_copy(owner, peer):
        where = noisy.at[at_rows(owner * rows, rows)]
        return remote(where, where, noi_s.at[peer], noi_r.at[owner], {"seq": peer})

    def text_copy(owner, peer):
        where = text.at[at_rows(owner * half, half)]
        return remote(where, where, txt_s.at[peer], txt_r.at[owner], {"seq": peer})

    def dp_copy(owner, peer):
        return remote(
            mod.at[:, pl.ds(0, 2 * width)],
            moddp.at[owner],
            dp_s.at[peer],
            dp_r.at[owner],
            {"dp": peer},
        )

    def region(first, count, p, s):
        return wall.at[pl.ds(first, count), at_rows(p * strip, strip), at_lanes(s * span, span)]

    def z_copy(owner, peer):
        where = region(owner, 1, mine, slot)
        return remote(where, where, wz_s.at[peer], wz_r.at[owner], {"seq": peer})

    def along(step):
        return lax.rem(mine + 2 * step + dps, dps)

    def x_near(step, origin, to):
        where = region(0, seqs, origin, slot)
        return remote(where, where, wx_s.at[step], wx_r.at[step], {"dp": to})

    def x_far(step, origin, to):
        where = region(step * (seqs // 2), seqs // 2, origin, slot)
        return remote(where, where, wx_s.at[2 + step], wx_r.at[2 + step], {"dp": to})

    def y_copy(which, side, origin, s):
        where = region(side * (seqs // 2), seqs // 2, origin, s)
        to = me if side == 0 else lax.rem(me + seqs // 2, seqs)
        return remote(
            where,
            where,
            wy_s.at[which * 2 + side],
            wy_r.at[which * 2 + side],
            {"pair": other, "seq": to},
        )

    sibling = mine + 1 - 2 * lax.rem(mine, 2)

    def c_copy(which, origin, s):
        where = region(0, seqs, origin, s)
        return remote(where, where, wc_s.at[which], wc_r.at[which], {"dp": sibling})

    def spread(which, origin):
        y_copy(which, 0, origin, slot).start()
        y_copy(which, 1, origin, slot).start()
        c_copy(which, origin, slot).start()

    def send_small(peer):
        mod_copy(me, peer).start()
        noisy_copy(me, peer).start()

    others(me, seqs, send_small)
    others(me, seqs, lambda peer: z_copy(me, peer).start())
    others(me, seqs, lambda peer: text_copy(me, peer).start())
    mod[:, at_lanes(me * part, part)] = mod_part

    emb_c = embed[...].astype(F32)
    emb_c = emb_c - row_mean(emb_c)
    e_top, e_rest = halves(emb_c)
    gram = stacked(mm_nt(e_top, e_top) + mm_nt(e_top, e_rest) + mm_nt(e_rest, e_top))

    others(me, seqs, lambda peer: mod_copy(peer, peer).wait_recv())
    shift_img, scale_img, shift_txt, scale_txt, shift_out, scale_out = [
        mod[:, i * width : (i + 1) * width] for i in range(6)
    ]
    moddp[mine] = mod[:, 0 : 2 * width]
    others(mine, dps, lambda peer: dp_copy(mine, peer).start())

    img_lhs = with_shift(emb_c * (1.0 + scale_img), shift_img)
    img_m = mm(img_lhs, wimg[...])
    img_m2 = stacked(img_m[0:ch])
    img_shift = img_m[ch : ch + 1] + img_m[ch + 1 : ch + 2]
    low_m = mm_nt(img_lhs, adown_t[...])
    low_m2 = stacked(low_m[0:ch])
    low_shift = low_m[ch : ch + 1] + low_m[ch + 1 : ch + 2]
    up = aup[:, at_lanes(me * 128, 128)]
    gain_q = qg[...]
    gain_k = kg[...]
    score_scale = math.log2(math.e) / math.sqrt(128.0)
    vext[:, 128:256] = jnp.ones((vext.shape[0], 128), BF16)

    others(me, seqs, lambda peer: noisy_copy(peer, peer).wait_recv())

    def project(i):
        here = at_rows(i * block, block)
        nb = noisy[here, :]
        nf = nb[:, 0:ch].astype(F32)
        var = jnp.sum(mm(nb, gram) * nf, -1, keepdims=True) * (1.0 / width)
        inv = lax.rsqrt(var + epsilon)
        qkv = mm(nb, img_m2) * inv + img_shift
        low = (mm(nb, low_m2) * inv + low_shift).astype(BF16)
        delta = mm(low, up).astype(BF16).astype(F32)
        q = qkv[:, 0:128]
        k = qkv[:, 128:256]
        q_pol = q + delta
        q2[here, :] = (q * rms_rows(q) * (gain_q * score_scale)).astype(BF16)
        q2[at_rows(images + i * block, block), :] = (
            q_pol * rms_rows(q_pol) * (gain_q * score_scale)
        ).astype(BF16)
        pol[here, :] = q_pol
        kk[here, :] = (k * rms_rows(k) * gain_k).astype(BF16)
        vext[here, 0:128] = qkv[:, 256:384].astype(BF16)
        lhs[here, :] = jnp.concatenate([low, (nf * inv).astype(BF16)], 1)

    each(blocks, project)

    others(me, seqs, lambda peer: z_copy(peer, peer).wait_recv())
    if ring > 1:
        x_near(0, mine, along(1)).start()
        x_near(1, mine, along(-1)).start()
    spread(0, mine)

    def attend(here, keys):
        s = mm_nt(q2[here, :], kk[keys, :])
        return mm(jnp.exp2(s).astype(BF16), vext[keys, :])

    def image_keys(i):
        here = at_rows(i * block, block)
        oacc[here, :] = attend(here, pl.ds(0, images))

    each(2 * blocks, image_keys)

    if ring > 1:
        x_near(0, along(-1), along(1)).wait_recv()
        x_far(0, along(-1), along(1)).start()
        spread(1, along(-1))
        x_near(1, along(1), along(-1)).wait_recv()
        x_far(1, along(1), along(-1)).start()
        spread(2, along(1))

    others(me, seqs, lambda peer: text_copy(peer, peer).wait_recv())
    text_n = (text[...].astype(F32) * (1.0 + scale_txt) + shift_txt).astype(BF16)
    kv = mm(text_n, wtxt[...])
    k = kv[:, 0:128]
    my_keys = at_rows(images + slot * texts, texts)
    kk[my_keys, :] = (k * rms_rows(k) * gain_k).astype(BF16)
    vext[my_keys, 0:128] = kv[:, 128:256].astype(BF16)

    def kv_copies(owner):
        keys = at_rows(images + owner * texts, texts)
        v = vext.at[keys, pl.ds(0, 128)]
        return (
            remote(kk.at[keys], kk.at[keys], kv_s.at[0], kv_r.at[0], {"pair": other}),
            remote(v, v, kv_s.at[1], kv_r.at[1], {"pair": other}),
        )

    for copy in kv_copies(slot):
        copy.start()
    for copy in kv_copies(other):
        copy.wait_recv()

    def out_copy(kind, owner, peer):
        return remote(
            outb.at[at_rows(kind * images + peer * rows, rows)],
            x.at[at_rows(kind * rows, rows), at_lanes(owner * 128, 128)],
            x_s.at[kind, peer],
            x_r.at[kind, owner],
            {"seq": peer},
        )

    def text_keys(i):
        kind = lax.div(i, blocks)
        b = lax.rem(i + lax.div(me, 4), blocks)
        here = at_rows(kind * images + b * block, block)
        o = oacc[here, :] + attend(here, pl.ds(images, 2 * texts))
        inv = 1.0 / o[:, 128:256]
        out = o[:, 0:128] * inv
        outb[here, :] = out.astype(BF16)

        @pl.when(kind == 1)
        def _():
            outf[at_rows(b * block, block), :] = out
            rl[at_rows(b * block, block), :] = inv

        for j in range(4):
            peer = b * 4 + j

            @pl.when(peer != me)
            def _():
                out_copy(kind, me, peer).start()

            @pl.when(peer == me)
            def _():
                x[at_rows(kind * rows, rows), at_lanes(me * 128, 128)] = outb[
                    at_rows(kind * images + me * rows, rows), :
                ]

    each(2 * blocks, text_keys)

    if ring > 1:
        x_far(0, along(2), along(1)).wait_recv()
        x_far(1, along(2), along(-1)).wait_recv()
        spread(3, along(2))
    for which in range(ring):
        origin = [mine, along(-1), along(1), along(2)][which]
        y_copy(which, 0, origin, other).wait_recv()
        y_copy(which, 1, origin, other).wait_recv()
        c_copy(4 + which, origin, other).start()
    for which in range(ring):
        origin = [sibling, lax.rem(sibling - 2 + dps, dps), lax.rem(sibling + 2, dps), lax.rem(sibling + 4, dps)][which]
        c_copy(which, origin, slot).wait_recv()
        c_copy(4 + which, origin, other).wait_recv()

    def finish_out(peer):
        for kind in range(2):
            out_copy(kind, peer, peer).wait_recv()

    others(me, seqs, finish_out)

    own = noisy[at_rows(me * rows, rows), :][:, 0:ch]
    tile = 256
    xv = x[...]

    def mix(i):
        here = at_lanes(i * tile, tile)
        states = mm(own, embed[:, here])
        w = wall[:, :, here].reshape(128 * seqs, tile)
        mixed[:, here] = mm(xv, w) + jnp.concatenate([states, states], 0)

    each(width // tile, mix)
    full = mixed[...]
    full = full - row_mean(full)
    inv = lax.rsqrt(row_mean(full * full) + epsilon)
    unit = full * inv
    mixed[...] = unit
    pred = mm_nt((unit * (1.0 + scale_out) + shift_out).astype(BF16), lw_t[...])
    target = noi[...].astype(F32) - lat[...].astype(F32)
    diff = jnp.concatenate([target, target], 0) - pred
    squares = diff * diff
    gap = (jnp.sum(squares[rows:]) - jnp.sum(squares[:rows])) * (1.0 / (images * ch))
    gapbuf[slot * seqs + me] = jnp.full((8, 128), gap, F32)

    def gap_copy(to_slot, from_slot, owner, peer):
        return remote(
            gapbuf.at[slot * seqs + me],
            gapbuf.at[from_slot * seqs + owner],
            e_s.at[to_slot * seqs + peer],
            e_r.at[from_slot * seqs + owner],
            {"seq": peer, "pair": to_slot},
        )

    g_ln = mm(diff[rows:].astype(BF16), lw_t[...]) * (1.0 + scale_out)
    unit_p = mixed[rows:, :]
    gmix[...] = (
        (g_ln - row_mean(g_ln) - unit_p * row_mean(g_ln * unit_p)) * inv[rows:]
    ).astype(BF16)

    def g_copy(owner, peer):
        return remote(
            ghs.at[peer],
            gh.at[at_rows(owner * rows, rows)],
            g_s.at[peer],
            g_r.at[owner],
            {"seq": peer},
        )

    def heads_back(i):
        pair = lax.rem(i + lax.div(me, 2), seqs // 2)
        w = wall[pl.ds(2 * pair, 2)].reshape(256, width)
        g = mm_nt(gmix[...], w).astype(BF16)
        for j in range(2):
            peer = 2 * pair + j
            ghs[peer] = g[:, j * 128 : (j + 1) * 128]

            @pl.when(peer != me)
            def _():
                g_copy(me, peer).start()

            @pl.when(peer == me)
            def _():
                gh[at_rows(me * rows, rows), :] = ghs[me]

    each(seqs // 2, heads_back)

    def send_gap(peer):
        gap_copy(slot, slot, me, peer).start()
        gap_copy(other, slot, me, peer).start()

    others(me, seqs, send_gap)
    gap_copy(other, slot, me, me).start()
    acc[...] = jnp.zeros_like(acc)
    csum[...] = jnp.zeros_like(csum)
    others(me, seqs, lambda peer: g_copy(peer, peer).wait_recv())
    keys = kk[...]
    vals = vext[:, 0:128]

    def back(i):
        here = at_rows(i * block, block)
        g = gh[here, :]
        p = jnp.exp2(mm_nt(q2[at_rows(images + i * block, block), :], keys))
        gp = mm_nt(g, vals)
        dsum = jnp.sum(g.astype(F32) * outf[here, :], -1, keepdims=True)
        gs = (p * (gp - dsum)).astype(BF16)
        gq = mm(gs, keys) * (rl[here, :] * (1.0 / math.sqrt(128.0)))
        u = pol[here, :]
        r = rms_rows(u)
        w = gq * gain_q
        gd = (r * w - u * (r * r * r) * row_mean(u * w)).astype(BF16)
        acc[...] += mm_tn(lhs[here, :], gd)
        csum[...] += jnp.broadcast_to(
            jnp.sum(gd.astype(F32), 0, keepdims=True), csum.shape
        )

    each(blocks, back)

    def finish(peer):
        mod_copy(me, peer).wait_send()
        noisy_copy(me, peer).wait_send()
        text_copy(me, peer).wait_send()
        z_copy(me, peer).wait_send()
        for kind in range(2):
            out_copy(kind, me, peer).wait_send()
        gap_copy(slot, slot, peer, peer).wait_recv()
        gap_copy(slot, other, peer, peer).wait_recv()
        gap_copy(slot, slot, me, peer).wait_send()
        gap_copy(other, slot, me, peer).wait_send()
        g_copy(me, peer).wait_send()

    others(me, seqs, finish)
    gap_copy(slot, other, me, me).wait_recv()
    gap_copy(other, slot, me, me).wait_send()

    def finish_dp(peer):
        dp_copy(mine, peer).wait_send()
        dp_copy(peer, peer).wait_recv()

    others(mine, dps, finish_dp)
    for copy in kv_copies(slot):
        copy.wait_send()
    if ring > 1:
        for step in range(2):
            x_near(step, mine, along(1)).wait_send()
            x_far(step, mine, along(1)).wait_send()
    for which in range(ring):
        for side in range(2):
            y_copy(which, side, mine, slot).wait_send()
        c_copy(which, mine, slot).wait_send()
        c_copy(4 + which, mine, slot).wait_send()

    own_gap = jnp.sum(gapbuf[pl.ds(slot * seqs, seqs)], 0)
    other_gap = jnp.sum(gapbuf[pl.ds(other * seqs, seqs)], 0)
    sgn = sign[0, 0]
    z = half_beta * sgn * (own_gap - other_gap)
    value[...] = jnp.maximum(z, 0.0) + jnp.log1p(jnp.exp(-jnp.abs(z)))
    weight = half_beta / dps / (1.0 + jnp.exp(-z))
    factor = (sgn * weight * (-2.0 / (images * ch)))[0:1, :]
    rank = up.shape[0]
    ua[0:rank, :] = (acc[0:rank, :] * factor).astype(BF16)
    a_top, a_rest = halves(jnp.concatenate([acc[rank : rank + ch, :], csum[...]], 0))
    tail = mm_nt(a_top, up) + mm_nt(a_rest, up)
    lower = jnp.concatenate([tail[0 : ch // 2], tail[ch // 2 : ch]], 1)
    lowest = jnp.concatenate([tail[ch:], tail[ch:]], 1)
    packed = jnp.concatenate([lower, lowest, lowest], 0) * factor
    ua[rank:, :] = packed.astype(BF16)


def last_kernel(
    seqs, dps, ua, embed, moddp,
    down_t, upg,
    ubuf, abuf, a2, usum, asum, left, right, upb,
    u_s, u_r, a_s, a_r, v_s, v_r, b_s, b_r,
):
    me = lax.axis_index("seq")
    slot = lax.axis_index("pair")
    mine = lax.axis_index("dp")
    width = embed.shape[1]
    ch = embed.shape[0]
    rank = upg.shape[0]
    tail = ua.shape[0] - rank
    reps = 2 * dps
    rep = slot * dps + mine
    barrier, total = greet([("seq", me, seqs)])

    def to(r):
        return {"pair": lax.div(r, dps), "dp": lax.rem(r, dps)}

    others(
        rep,
        reps,
        lambda peer: pl.semaphore_signal(
            barrier, inc=1, device_id=to(peer), device_id_type=pl.DeviceIdType.MESH
        ),
    )
    pl.semaphore_wait(barrier, total + reps - 1)

    def u_copy(owner, peer):
        return remote(
            ua.at[pl.ds(0, rank)], ubuf.at[owner], u_s.at[peer], u_r.at[owner], to(peer)
        )

    def a_copy(owner, peer):
        return remote(
            ua.at[pl.ds(rank, tail)], abuf.at[owner], a_s.at[peer], a_r.at[owner], {"seq": peer}
        )

    def v_copy(owner, peer):
        return remote(
            usum,
            upb.at[:, at_lanes(owner * 128, 128)],
            v_s.at[peer],
            v_r.at[owner],
            {"seq": peer},
        )

    def b_copy(owner, peer):
        return remote(asum, a2.at[owner], b_s.at[peer], b_r.at[owner], to(peer))

    others(rep, reps, lambda peer: u_copy(rep, peer).start())
    others(me, seqs, lambda peer: a_copy(me, peer).start())
    ubuf[rep] = ua[0:rank, :]
    abuf[me] = ua[rank:, :]
    emb_c = embed[...].astype(F32)
    emb_c = emb_c - row_mean(emb_c)
    first = lax.broadcasted_iota(jnp.int32, (16, width), 0) == 0
    deep = ch + 16
    for p in range(dps):
        shift = moddp[p, :, 0:width]
        scale = moddp[p, :, width:]
        scaled = emb_c * (1.0 + scale)
        extra = jnp.where(first, shift, 0.0)
        left[p * deep : (p + 1) * deep, :] = jnp.concatenate([scaled, extra], 0).astype(BF16)
    others(rep, reps, lambda peer: u_copy(peer, peer).wait_recv())
    sums = jnp.sum(ubuf[...].astype(F32), 0).astype(BF16)
    usum[...] = sums
    upb[:, at_lanes(me * 128, 128)] = sums
    others(me, seqs, lambda peer: v_copy(me, peer).start())
    others(me, seqs, lambda peer: a_copy(peer, peer).wait_recv())
    sums = jnp.sum(abuf[...].astype(F32), 0).astype(BF16)
    asum[...] = sums
    a2[rep] = sums
    others(rep, reps, lambda peer: b_copy(rep, peer).start())
    others(rep, reps, lambda peer: b_copy(peer, peer).wait_recv())
    for p in range(dps):
        a = a2[p].astype(F32) + a2[dps + p].astype(F32)
        top = a[0 : ch // 2]
        right[p * deep : (p + 1) * deep, :] = jnp.concatenate(
            [top[:, 0:ch], top[:, ch:], a[ch // 2 :, 0:ch]], 0
        ).astype(BF16)
    down_t[...] = mm_tn(right[...], left[...])

    def finish(peer):
        a_copy(me, peer).wait_send()
        v_copy(me, peer).wait_send()
        v_copy(peer, peer).wait_recv()

    others(me, seqs, finish)
    upg[...] = upb[...].astype(F32)

    def finish_reps(peer):
        u_copy(rep, peer).wait_send()
        b_copy(rep, peer).wait_send()

    others(rep, reps, finish_reps)


def shape(dims, kind):
    return jax.ShapeDtypeStruct(dims, kind)


def call(kernel, ident, specs, outs, scratch, cost, *operands):
    return pl.pallas_call(
        kernel,
        out_shape=outs,
        in_specs=[pl.BlockSpec(memory_space=s) for s in specs],
        out_specs=[pl.BlockSpec(memory_space=pltpu.VMEM)] * len(outs),
        scratch_shapes=scratch,
        compiler_params=pltpu.CompilerParams(
            collective_id=ident, has_side_effects=True, vmem_limit_bytes=VMEM_BYTES
        ),
        cost_estimate=pl.CostEstimate(flops=cost, bytes_accessed=16 << 20, transcendentals=0),
    )(*operands)


def on_device(
    latents,
    noise,
    pair_timestep_index,
    preferred_image_slot,
    prompt_token_states,
    image_embed_weight,
    timestep_modulation_weight,
    image_query_key_value,
    text_key_value,
    query_norm_gain,
    key_norm_gain,
    adapter_down_weight,
    adapter_up_weight,
    image_output_weight,
    latent_out_weight,
):
    seqs = lax.axis_size("seq")
    dps = lax.axis_size("dp")
    slot = lax.axis_index("pair")
    rows, ch = latents.shape[2:]
    images = rows * seqs
    width = image_embed_weight.shape[1]
    texts = prompt_token_states.shape[1] * seqs
    keys = images + texts
    rank = adapter_down_weight.shape[1]
    step_value = pair_timestep_index[0].astype(jnp.float32)
    level = ((step_value + 1.0) / horizon).reshape(1, 1)
    emb = jnp.broadcast_to(
        sinusoid(step_value, timestep_modulation_weight.shape[0]).astype(BF16)[None],
        (16, timestep_modulation_weight.shape[0]),
    )
    lat = latents[0, 0]
    noi = noise[0]

    sign = jnp.where(preferred_image_slot[0] == slot, 1.0, -1.0).astype(F32).reshape(1, 1)
    V, S = pltpu.VMEM, pltpu.SMEM
    DMA = pltpu.SemaphoreType.DMA
    tail = ch // 2 + 16
    heads = 128 * seqs
    scratch = [
        V((1, 6 * width), F32),
        V((images, 128), BF16),
        V((texts // 2, width), BF16),
        V((2 * images, 256), F32),
        V((2 * images, 128), BF16),
        V((2 * images, 128), BF16),
        V((1, timestep_modulation_weight.shape[1]), F32),
        V((2 * rows, heads), BF16),
        V((seqs, 128, width), BF16),
        V((keys, 128), BF16),
        V((keys, 256), BF16),
        V((images, 128), F32),
        V((images, 128), BF16),
        V((images, 128), F32),
        V((images, 128), F32),
        V((2 * rows, width), F32),
        V((rows, width), BF16),
        V((images, 128), BF16),
        V((seqs, rows, 128), BF16),
        V((2 * seqs, 8, 128), F32),
        V((rank + ch, 128), F32),
        V((8, 128), F32),
    ]
    scratch += [DMA((seqs,))] * 6 + [DMA((dps,))] * 2 + [DMA((2,))] * 2 + [DMA((2, seqs))] * 2
    scratch += [DMA((seqs,))] * 2 + [DMA((2 * seqs,))] * 2 + [DMA((seqs,))] * 2
    scratch += [DMA((4,))] * 2 + [DMA((8,))] * 4
    ua, value, moddp = call(
        functools.partial(main_kernel, seqs, dps),
        0,
        [S, S] + [V] * 14,
        [
            shape((rank + tail, 128), BF16),
            shape((8, 128), F32),
            shape((dps, 1, 2 * width), F32),
        ],
        scratch,
        30 * 10**9,
        level,
        sign,
        emb,
        lat,
        noi,
        prompt_token_states[0],
        image_embed_weight,
        timestep_modulation_weight,
        image_query_key_value.reshape(width, -1),
        text_key_value.reshape(width, -1),
        query_norm_gain.reshape(1, -1),
        key_norm_gain.reshape(1, -1),
        adapter_down_weight.T,
        adapter_up_weight,
        image_output_weight,
        latent_out_weight.T,
    )
    reps = 2 * dps
    deep = ch + 16
    scratch = [
        V((reps, rank, 128), BF16),
        V((seqs, tail, 128), BF16),
        V((reps, tail, 128), BF16),
        V((rank, 128), BF16),
        V((tail, 128), BF16),
        V((dps * deep, width), BF16),
        V((dps * deep, ch), BF16),
        V((rank, heads), BF16),
    ]
    scratch += [DMA((reps,))] * 2 + [DMA((seqs,))] * 4 + [DMA((reps,))] * 2
    down_t, upg = call(
        functools.partial(last_kernel, seqs, dps),
        1,
        [V] * 3,
        [shape((ch, width), F32), shape((rank, heads), F32)],
        scratch,
        10**9,
        ua,
        image_embed_weight,
        moddp,
    )
    return (down_t.T, upg, value[0, 0:1])


def solution(mesh):
    return jax.shard_map(
        on_device,
        mesh=mesh,
        in_specs=(
            P("dp", "pair", "seq", None),
            P("dp", "seq", None),
            P("dp"),
            P("dp"),
            P("dp", "seq", None),
            P(),
            P(None, "seq"),
            P(None, "seq", None),
            P(None, "seq", None),
            P(),
            P(),
            P(),
            P(),
            P("seq", None),
            P(),
        ),
        out_specs=(P(), P(), P("dp")),
        check_vma=False,
    )
```

time: 283 us -> 178 us (0.63)
  blocking collectives: 39.7 us -> 0 us
  Pallas kernels: 195 us -> 167 us
  between operations: 15.5 us -> 1.96 us
  starting transfers between devices: 11.1 us -> 0 us
  waiting for transfers between devices: 9.65 us -> 0 us
  other arithmetic: 3.35 us -> 0.06 us
    all_gather x1 -> x0, blocking collectives: 39.7 us -> none  [on_device(): kb = lax.all_gather(mm_nt(wo_c, wo_other).astype(BF16), 'seq')]
    pallas_call x3 -> x2, Pallas kernels: 195 us -> 167 us  [call(): pl.pallas_call(kernel, out_shape=outs, in_specs=[pl.BlockSpec(memory_spac...]
    ppermute x1 -> x0, starting transfers between devices: 11.1 us -> none  [on_device(): wo_other = lax.ppermute(wo_c, everyone, moves)]
    ppermute x1 -> x0, waiting for transfers between devices: 9.61 us -> none  [on_device(): wo_other = lax.ppermute(wo_c, everyone, moves)]
    unnamed x20 -> x4, local copies, waits for them, and re-layouts: 6.22 us -> 6.78 us
  transfers between devices with their start and end apart: 2 -> 0, of which waited for: 1 -> 0; matrix products, arithmetic and copies ran while one was open for 1% -> 0% of each run, Pallas kernels for 43% -> 0%
where the time goes in v2:
time: 178 us
  Pallas kernels  167 us (94%)
  local copies, waits for them, and re-layouts  8.56 us (5%)
  between operations  1.96 us (1%)
    pallas_call x2, Pallas kernels, call(): pl.pallas_call(kernel, out_shape=outs, in_specs=[pl.BlockSpec(memory_spac...  167 us
    unnamed x4, local copies, waits for them, and re-layouts  6.78 us

profile of v2, /device:TPU:1, one launch (start us, length us, event | category | flops | bytes accessed | tf_op | source)
XLA Modules:
  0.0 177.8 jit_solution(13109211467391946533)
XLA Ops:
  1.9 0.1 sine_convert_fusion
  2.0 0.6 broadcast_in_dim.2.emb
  2.6 1.4 copy.18
  4.0 1.4 copy.19
  5.4 143.7 %shard_map.166 = (bf16[112,128]{1,0:T(8,128)(2,1)}, f32[8,128]{1,0:T(8,128)}, f32[8,1,6144]{2,1,0:T(1,128)}) custom-call(f32[1,1]{1,0:T(1,128)} %bitcast.1.level, f32[1,1]{1,0:T(1,128)} %bitcast.3.sign, bf16[16,256]{1,0:T(8,128)(2,1)} %broadcast_in_dim.2.emb, bf16[96,64]{1,0:T(8,128)(2,1)} %bitcast.17, bf16[96,64]{1,0:T(8,128)(2,1)} %bitcast.18, ...), custom_call_target="tpu_custom_call" | custom-call | flops 30000001024 | bytes 16777216 | tf_op jit(solution)/shard_map/pallas_call | solution.py:646
  149.2 1.2 slice.3
  150.4 23.5 %shard_map.167 = (f32[64,3072]{1,0:T(8,128)}, f32[64,2048]{1,0:T(8,128)}) custom-call(bf16[112,128]{1,0:T(8,128)(2,1)} %get-tuple-element.8.ua, bf16[64,3072]{1,0:T(8,128)(2,1)} %embed.3, f32[8,1,6144]{2,1,0:T(1,128)} %get-tuple-element.9.moddp), custom_call_target="tpu_custom_call" | custom-call | flops 1000000000 | bytes 16777216 | tf_op jit(solution)/shard_map/pallas_call | solution.py:646
  173.9 2.1 %copy.24 = f32[3072,64]{0,1:T(8,128)} copy(f32[3072,64]{0,1:T(8,128)} %bitcast.16) | data formatting | bytes 1572864
  175.9 1.9 %copy.25 = f32[64,2048]{1,0:T(8,128)} copy(f32[64,2048]{1,0:T(8,128)} %get-tuple-element.19) | data formatting | bytes 1048576
  (1 shorter events, 0.0 us)

commit v3 on v2

v3 whole, which is shorter than its diff:
```python
import functools
import math

import jax
import jax.numpy as jnp
from jax import lax
from jax.experimental import pallas as pl
from jax.experimental.pallas import tpu as pltpu
from jax.sharding import PartitionSpec as P

epsilon = 1e-06
half_beta = 20.0
horizon = 1000.0
F32 = jnp.float32
BF16 = jnp.bfloat16
VMEM_BYTES = 58 * 1024 * 1024


def sinusoid(step_value, width):
    half_width = width // 2
    freqs = jnp.exp(-math.log(10000.0) * jnp.arange(half_width, dtype=jnp.float32) / half_width)
    angle = step_value * freqs
    return jnp.concatenate([jnp.cos(angle), jnp.sin(angle)])


def mm(a, b):
    return lax.dot_general(a, b, (((1,), (0,)), ((), ())), preferred_element_type=F32)


def mm_nt(a, b):
    return lax.dot_general(a, b, (((1,), (1,)), ((), ())), preferred_element_type=F32)


def mm_tn(a, b):
    return lax.dot_general(a, b, (((0,), (0,)), ((), ())), preferred_element_type=F32)


def halves(a):
    top = a.astype(BF16)
    return top, (a - top.astype(F32)).astype(BF16)


def stacked(a):
    top, rest = halves(a)
    return jnp.concatenate([top, rest], 0)


def row_mean(a):
    return jnp.mean(a, -1, keepdims=True)


def rms_rows(rows):
    return lax.rsqrt(row_mean(rows * rows) + epsilon)


def remote(src, dst, send, recv, device):
    return pltpu.make_async_remote_copy(
        src_ref=src,
        dst_ref=dst,
        send_sem=send,
        recv_sem=recv,
        device_id=device,
        device_id_type=pl.DeviceIdType.MESH,
    )


def each(count, body):
    @pl.loop(0, count)
    def _(i):
        body(i)


def others(me, count, body):
    @pl.loop(1, count)
    def _(step):
        body(lax.rem(me + step, count))


def greet(axes):
    barrier = pltpu.get_barrier_semaphore()
    total = 0
    for axis, me, count in axes:
        others(
            me,
            count,
            lambda peer: pl.semaphore_signal(
                barrier,
                inc=1,
                device_id={axis: peer},
                device_id_type=pl.DeviceIdType.MESH,
            ),
        )
        total += count - 1
    return barrier, total


def at_rows(start, size):
    return pl.ds(pl.multiple_of(start, 16), size)


def at_lanes(start, size):
    return pl.ds(pl.multiple_of(start, 128), size)


def with_shift(scaled, shift):
    width = shift.shape[1]
    top, rest = halves(shift)
    which = lax.broadcasted_iota(jnp.int32, (16, width), 0)
    extra = jnp.where(
        which == 0,
        top.astype(F32),
        jnp.where(which == 1, rest.astype(F32), 0.0),
    )
    return jnp.concatenate([scaled, extra], 0).astype(BF16)


def main_kernel(
    seqs, dps, step, pref, emb, lat_t, noi_t, txt, embed, wmod, wimg, wtxt, qg, kg, adown_t, aup, wo, lw_t,
    down, upb, value,
    wimg_v, wtxt_v, mod, moddp, noisy, text, oacc, q2, outb, modrow, x, wall, kk, vext, pol, lhs, outf, rl,
    mixed, gmix, gh, ghs, gapbuf, acc, csum, ua, ubuf, abuf, a2, usum, asum, left, right,
    in_s, mod_s, mod_r, noi_s, noi_r, txt_s, txt_r, dp_s, dp_r, kv_s, kv_r, x_s, x_r,
    g_s, g_r, e_s, e_r, wz_s, wz_r, wx_s, wx_r, wy_s, wy_r, wc_s, wc_r,
    u_s, u_r, a_s, a_r, v_s, v_r, b_s, b_r,
):
    me = lax.axis_index("seq")
    slot = lax.axis_index("pair")
    mine = lax.axis_index("dp")
    other = 1 - slot
    ch, rows = lat_t.shape
    images = rows * seqs
    width = embed.shape[1]
    span = width // 2
    strip = 128 // dps
    origins = dps // 2
    half = txt.shape[0] // 2
    texts = half * seqs
    block = 4 * rows
    blocks = images // block
    part = wmod.shape[1]
    zs = seqs // 2
    z_at, hi = lax.rem(me, zs), lax.div(me, zs)
    flip = lax.rem(me + zs, seqs)
    reps = 2 * dps
    rep = slot * dps + mine

    loads = [
        pltpu.make_async_copy(
            wo.at[at_rows(mine * strip, strip), at_lanes(slot * span, span)],
            wall.at[me, at_rows(mine * strip, strip), at_lanes(slot * span, span)],
            in_s.at[0],
        ),
        pltpu.make_async_copy(wimg, wimg_v, in_s.at[1]),
        pltpu.make_async_copy(wtxt, wtxt_v, in_s.at[2]),
    ]
    for load in loads:
        load.start()
    barrier, total = greet([("seq", me, seqs), ("dp", mine, dps)])
    total += seqs + dps - 1

    def greet_other(device):
        pl.semaphore_signal(
            barrier, inc=1, device_id=device, device_id_type=pl.DeviceIdType.MESH
        )

    each(seqs, lambda peer: greet_other({"seq": peer, "pair": other}))
    others(mine, dps, lambda peer: greet_other({"dp": peer, "pair": other}))

    mod_part = mm(jnp.broadcast_to(emb[...].astype(F32), (16, emb.shape[1])).astype(BF16), wmod[...])[0:1]
    modrow[...] = mod_part
    lev = (step[0].astype(F32) + 1.0) * (1.0 / horizon)
    lat_f = lat_t[...].astype(F32)
    noi_f = noi_t[...].astype(F32)
    own = ((1.0 - lev) * lat_f + lev * noi_f).T.astype(BF16)
    target = (noi_f - lat_f).T
    noisy[me] = jnp.concatenate([own[0 : rows // 2], own[rows // 2 :]], 1)
    t = txt[at_rows(slot * half, half), :].astype(F32)
    t = t - row_mean(t)
    text[at_rows(me * half, half), :] = (t * lax.rsqrt(row_mean(t * t) + epsilon)).astype(BF16)
    loads[0].wait()
    pl.semaphore_wait(barrier, total)

    def mod_copy(owner, peer):
        return remote(
            modrow,
            mod.at[:, at_lanes(owner * part, part)],
            mod_s.at[peer],
            mod_r.at[owner],
            {"seq": peer},
        )

    def noisy_copy(owner, peer):
        where = noisy.at[owner]
        return remote(where, where, noi_s.at[peer], noi_r.at[owner], {"seq": peer})

    def dp_copy(owner, peer):
        return remote(
            mod.at[:, pl.ds(0, 2 * width)],
            moddp.at[owner],
            dp_s.at[peer],
            dp_r.at[owner],
            {"dp": peer},
        )

    def region(first, count, p, s):
        return wall.at[pl.ds(first, count), at_rows(p * strip, strip), at_lanes(s * span, span)]

    def owner_at(h, away):
        return h * zs + lax.rem(z_at + away + zs, zs)

    right_z, left_z = owner_at(hi, 1), owner_at(hi, -1)

    def ring_copy(kind, lane, owner, to):
        if kind == 0:
            where, send, recv = region(owner, 1, mine, slot), wz_s, wz_r
        else:
            where, send, recv = text.at[at_rows(owner * half, half)], txt_s, txt_r
        return remote(where, where, send.at[lane * seqs + owner], recv.at[owner], {"seq": to})

    def ring_sends(kind, hop):
        last = hop == zs // 2
        sends = []
        for h in range(2):
            if not last or h == 0:
                sends.append(ring_copy(kind, 1, owner_at(h, 1 - hop), right_z))
            if not last or h == 1:
                sends.append(ring_copy(kind, 2, owner_at(h, hop - 1), left_z))
        return sends

    def ring_first(kind):
        ring_copy(kind, 0, me, flip).start()
        if zs > 2:
            ring_copy(kind, 1, me, right_z).start()
            ring_copy(kind, 2, me, left_z).start()

    def ring_hop(kind, hop):
        if hop == 1:
            ring_copy(kind, 0, flip, flip).wait_recv()
            if zs > 2:
                ring_copy(kind, 1, flip, right_z).start()
                ring_copy(kind, 2, flip, left_z).start()
                return
        else:
            for h in range(2):
                ring_copy(kind, 0, owner_at(h, 1 - hop), flip).wait_recv()
                ring_copy(kind, 0, owner_at(h, hop - 1), flip).wait_recv()
        for copy in ring_sends(kind, hop):
            copy.start()

    def ring_end(kind):
        ring_copy(kind, 0, owner_at(0, zs // 2), flip).wait_recv()
        ring_copy(kind, 0, owner_at(1, zs // 2), flip).wait_recv()

    def ring_sent(kind):
        ring_copy(kind, 0, me, flip).wait_send()
        for hop in range(1, zs // 2 + 1):
            for copy in ring_sends(kind, hop):
                copy.wait_send()

    hops = zs // 2

    def along(away):
        return lax.rem(mine + 2 * away + dps, dps)

    places = [mine, along(-1), along(1), along(2)]
    sibling = mine + 1 - 2 * lax.rem(mine, 2)

    def chunk(origin, which_half, s):
        return region(which_half * (seqs // 2), seqs // 2, origin, s)

    def x_near(way, turn, origin):
        where = chunk(origin, turn if way == 0 else 1 - turn, slot)
        at = way * 2 + turn
        return remote(where, where, wx_s.at[at], wx_r.at[at], {"dp": along(1 - 2 * way)})

    def x_far(way, origin):
        where = chunk(origin, way, slot)
        return remote(where, where, wx_s.at[4 + way], wx_r.at[4 + way], {"dp": along(1 - 2 * way)})

    def y_copy(which, side, s):
        where = chunk(places[which], side, s)
        to = me if side == 0 else flip
        at = which * 2 + side
        return remote(where, where, wy_s.at[at], wy_r.at[at], {"pair": other, "seq": to})

    def c_copy(foreign, which, side, at_sibling):
        origin = places[which]
        if at_sibling:
            origin = sibling - mine + origin
        where = chunk(origin, side, other if foreign else slot)
        at = (foreign * 4 + which) * 2 + side
        return remote(where, where, wc_s.at[at], wc_r.at[at], {"dp": sibling})

    def spread(which, side):
        y_copy(which, side, slot).start()
        c_copy(0, which, side, False).start()

    def relay(which):
        for side in range(2):
            y_copy(which, side, other).wait_recv()
            c_copy(1, which, side, False).start()

    def send_small(peer):
        mod_copy(me, peer).start()
        noisy_copy(me, peer).start()

    others(me, seqs, send_small)
    ring_first(0)
    mod[:, at_lanes(me * part, part)] = mod_part

    emb_c = embed[...].astype(F32)
    emb_c = emb_c - row_mean(emb_c)
    e_top, e_rest = halves(emb_c)
    gram = stacked(mm_nt(e_top, e_top) + mm_nt(e_top, e_rest) + mm_nt(e_rest, e_top))
    ring_hop(0, 1)

    others(me, seqs, lambda peer: mod_copy(peer, peer).wait_recv())
    shift_img, scale_img, shift_txt, scale_txt, shift_out, scale_out = [
        mod[:, i * width : (i + 1) * width] for i in range(6)
    ]
    moddp[mine] = mod[:, 0 : 2 * width]
    others(mine, dps, lambda peer: dp_copy(mine, peer).start())
    if hops > 1:
        ring_hop(0, 2)

    loads[1].wait()
    img_lhs = with_shift(emb_c * (1.0 + scale_img), shift_img)
    img_m = mm(img_lhs, wimg_v[...])
    img_m2 = stacked(img_m[0:ch])
    img_shift = img_m[ch : ch + 1] + img_m[ch + 1 : ch + 2]
    low_m = mm_nt(img_lhs, adown_t[...])
    low_m2 = stacked(low_m[0:ch])
    low_shift = low_m[ch : ch + 1] + low_m[ch + 1 : ch + 2]
    up = aup[:, at_lanes(me * 128, 128)]
    gain_q = qg[...]
    gain_k = kg[...]
    score_scale = math.log2(math.e) / math.sqrt(128.0)
    vext[:, 128:256] = jnp.ones((vext.shape[0], 128), BF16)
    if hops > 2:
        ring_hop(0, 3)

    others(me, seqs, lambda peer: noisy_copy(peer, peer).wait_recv())

    def project(i):
        here = at_rows(i * block, block)
        pieces = []
        for j in range(4):
            packed = noisy[i * 4 + j]
            pieces += [packed[:, 0:ch], packed[:, ch:]]
        nb = jnp.concatenate(pieces, 0)
        nf = nb.astype(F32)
        nb = jnp.concatenate([nb, nb], 1)
        var = jnp.sum(mm(nb, gram) * nf, -1, keepdims=True) * (1.0 / width)
        inv = lax.rsqrt(var + epsilon)
        qkv = mm(nb, img_m2) * inv + img_shift
        low = (mm(nb, low_m2) * inv + low_shift).astype(BF16)
        delta = mm(low, up).astype(BF16).astype(F32)
        q = qkv[:, 0:128]
        k = qkv[:, 128:256]
        q_pol = q + delta
        q2[here, :] = (q * rms_rows(q) * (gain_q * score_scale)).astype(BF16)
        q2[at_rows(images + i * block, block), :] = (
            q_pol * rms_rows(q_pol) * (gain_q * score_scale)
        ).astype(BF16)
        pol[here, :] = q_pol
        kk[here, :] = (k * rms_rows(k) * gain_k).astype(BF16)
        vext[here, 0:128] = qkv[:, 256:384].astype(BF16)
        lhs[here, :] = jnp.concatenate([low, (nf * inv).astype(BF16)], 1)

    def spans(start, stop, body):
        @pl.loop(start, stop)
        def _(i):
            body(i)

    spans(0, blocks // 2, project)
    if hops > 3:
        ring_hop(0, 4)
    ring_first(1)
    spans(blocks // 2, blocks, project)
    ring_end(0)
    if origins > 1:
        for turn in range(2):
            for way in range(2):
                x_near(way, turn, mine).start()
    spread(0, 0)
    spread(0, 1)
    ring_hop(1, 1)

    def attend(here, keys):
        s = mm_nt(q2[here, :], kk[keys, :])
        return mm(jnp.exp2(s).astype(BF16), vext[keys, :])

    def image_keys(i):
        here = at_rows(i * block, block)
        oacc[here, :] = attend(here, pl.ds(0, images))

    spans(0, blocks // 2, image_keys)
    if hops > 1:
        ring_hop(1, 2)
    spans(blocks // 2, blocks, image_keys)
    if origins > 1:
        x_near(0, 0, places[1]).wait_recv()
        x_far(0, places[1]).start()
        spread(1, 0)
        x_near(1, 0, places[2]).wait_recv()
        x_far(1, places[2]).start()
        spread(2, 1)
    if hops > 2:
        ring_hop(1, 3)
    spans(blocks, 2 * blocks, image_keys)
    relay(0)
    if hops > 3:
        ring_hop(1, 4)
    if origins > 1:
        x_near(0, 1, places[1]).wait_recv()
        spread(1, 1)
        x_near(1, 1, places[2]).wait_recv()
        spread(2, 0)

    ring_end(1)
    loads[2].wait()
    text_n = (text[...].astype(F32) * (1.0 + scale_txt) + shift_txt).astype(BF16)
    kv = mm(text_n, wtxt_v[...])
    k = kv[:, 0:128]
    my_keys = at_rows(images + slot * texts, texts)
    kk[my_keys, :] = (k * rms_rows(k) * gain_k).astype(BF16)
    vext[my_keys, 0:128] = kv[:, 128:256].astype(BF16)

    def kv_copies(owner):
        keys = at_rows(images + owner * texts, texts)
        v = vext.at[keys, pl.ds(0, 128)]
        return (
            remote(kk.at[keys], kk.at[keys], kv_s.at[0], kv_r.at[0], {"pair": other}),
            remote(v, v, kv_s.at[1], kv_r.at[1], {"pair": other}),
        )

    for copy in kv_copies(slot):
        copy.start()
    for copy in kv_copies(other):
        copy.wait_recv()

    def out_copy(kind, owner, peer):
        return remote(
            outb.at[at_rows(kind * images + peer * rows, rows)],
            x.at[at_rows(kind * rows, rows), at_lanes(owner * 128, 128)],
            x_s.at[kind, peer],
            x_r.at[kind, owner],
            {"seq": peer},
        )

    def text_keys(i):
        kind = lax.div(i, blocks)
        b = lax.rem(i + lax.div(me, 4), blocks)
        here = at_rows(kind * images + b * block, block)
        o = oacc[here, :] + attend(here, pl.ds(images, 2 * texts))
        inv = 1.0 / o[:, 128:256]
        out = o[:, 0:128] * inv
        outb[here, :] = out.astype(BF16)

        @pl.when(kind == 1)
        def _():
            outf[at_rows(b * block, block), :] = out
            rl[at_rows(b * block, block), :] = inv

        for j in range(4):
            peer = b * 4 + j

            @pl.when(peer != me)
            def _():
                out_copy(kind, me, peer).start()

            @pl.when(peer == me)
            def _():
                x[at_rows(kind * rows, rows), at_lanes(me * 128, 128)] = outb[
                    at_rows(kind * images + me * rows, rows), :
                ]

    spans(0, 2 * blocks, text_keys)

    if origins > 1:
        x_far(0, places[3]).wait_recv()
        spread(3, 0)
        x_far(1, places[3]).wait_recv()
        spread(3, 1)
        relay(1)
        relay(2)

    def finish_dp(peer):
        dp_copy(mine, peer).wait_send()
        dp_copy(peer, peer).wait_recv()

    others(mine, dps, finish_dp)
    first = lax.broadcasted_iota(jnp.int32, (16, width), 0) == 0
    deep = ch + 16

    def build(p):
        shift = moddp[p, :, 0:width]
        scale = moddp[p, :, width:]
        extra = jnp.where(first, shift, 0.0)
        left[at_rows(p * deep, deep), :] = jnp.concatenate(
            [emb_c * (1.0 + scale), extra], 0
        ).astype(BF16)

    for p in range(dps):
        build(p)
    acc[...] = jnp.zeros_like(acc)
    csum[...] = jnp.zeros_like(csum)
    if origins > 1:
        relay(3)

    def finish_out(peer):
        for kind in range(2):
            out_copy(kind, peer, peer).wait_recv()

    others(me, seqs, finish_out)
    for which in range(origins):
        for side in range(2):
            c_copy(0, which, side, True).wait_recv()
            c_copy(1, which, side, True).wait_recv()

    tile = 256
    xv = x[...]

    def mix(i):
        here = at_lanes(i * tile, tile)
        states = mm(own, embed[:, here])
        w = wall[:, :, here].reshape(128 * seqs, tile)
        mixed[:, here] = mm(xv, w) + jnp.concatenate([states, states], 0)

    each(width // tile, mix)
    full = mixed[...]
    full = full - row_mean(full)
    inv = lax.rsqrt(row_mean(full * full) + epsilon)
    unit = full * inv
    mixed[...] = unit
    pred = mm_nt((unit * (1.0 + scale_out) + shift_out).astype(BF16), lw_t[...])
    diff = jnp.concatenate([target, target], 0) - pred
    squares = diff * diff
    gap = (jnp.sum(squares[rows:]) - jnp.sum(squares[:rows])) * (1.0 / (images * ch))
    gapbuf[slot * seqs + me] = jnp.full((8, 128), gap, F32)

    def gap_copy(to_slot, from_slot, owner, peer):
        return remote(
            gapbuf.at[slot * seqs + me],
            gapbuf.at[from_slot * seqs + owner],
            e_s.at[to_slot * seqs + peer],
            e_r.at[from_slot * seqs + owner],
            {"seq": peer, "pair": to_slot},
        )

    g_ln = mm(diff[rows:].astype(BF16), lw_t[...]) * (1.0 + scale_out)
    unit_p = mixed[rows:, :]
    gmix[...] = (
        (g_ln - row_mean(g_ln) - unit_p * row_mean(g_ln * unit_p)) * inv[rows:]
    ).astype(BF16)

    def g_copy(owner, peer):
        return remote(
            ghs.at[peer],
            gh.at[at_rows(owner * rows, rows)],
            g_s.at[peer],
            g_r.at[owner],
            {"seq": peer},
        )

    def heads_back(i):
        pair = lax.rem(i + lax.div(me, 2), seqs // 2)
        w = wall[pl.ds(2 * pair, 2)].reshape(256, width)
        g = mm_nt(gmix[...], w).astype(BF16)
        for j in range(2):
            peer = 2 * pair + j
            ghs[peer] = g[:, j * 128 : (j + 1) * 128]

            @pl.when(peer != me)
            def _():
                g_copy(me, peer).start()

            @pl.when(peer == me)
            def _():
                gh[at_rows(me * rows, rows), :] = ghs[me]

    each(seqs // 2, heads_back)

    def send_gap(peer):
        gap_copy(slot, slot, me, peer).start()
        gap_copy(other, slot, me, peer).start()

    others(me, seqs, send_gap)
    gap_copy(other, slot, me, me).start()
    keys = kk[...]
    vals = vext[:, 0:128]

    def back(i):
        b = lax.rem(i + lax.div(me, 4), blocks)
        for j in range(4):
            peer = b * 4 + j

            @pl.when(peer != me)
            def _():
                g_copy(peer, peer).wait_recv()

        here = at_rows(b * block, block)
        g = gh[here, :]
        p = jnp.exp2(mm_nt(q2[at_rows(images + b * block, block), :], keys))
        gp = mm_nt(g, vals)
        dsum = jnp.sum(g.astype(F32) * outf[here, :], -1, keepdims=True)
        gs = (p * (gp - dsum)).astype(BF16)
        gq = mm(gs, keys) * (rl[here, :] * (1.0 / math.sqrt(128.0)))
        u = pol[here, :]
        r = rms_rows(u)
        w = gq * gain_q
        gd = (r * w - u * (r * r * r) * row_mean(u * w)).astype(BF16)
        acc[...] += mm_tn(lhs[here, :], gd)
        csum[...] += jnp.broadcast_to(
            jnp.sum(gd.astype(F32), 0, keepdims=True), csum.shape
        )

    each(blocks, back)

    def wait_gap(peer):
        gap_copy(slot, slot, peer, peer).wait_recv()
        gap_copy(slot, other, peer, peer).wait_recv()

    others(me, seqs, wait_gap)
    gap_copy(slot, other, me, me).wait_recv()
    own_gap = jnp.sum(gapbuf[pl.ds(slot * seqs, seqs)], 0)
    other_gap = jnp.sum(gapbuf[pl.ds(other * seqs, seqs)], 0)
    sgn = (1.0 - 2.0 * pref[0].astype(F32)) * (1.0 - 2.0 * slot.astype(F32))
    z = half_beta * sgn * (own_gap - other_gap)
    value[...] = (jnp.maximum(z, 0.0) + jnp.log1p(jnp.exp(-jnp.abs(z))))[0:1, 0:1]
    weight = half_beta / dps / (1.0 + jnp.exp(-z))
    factor = (sgn * weight * (-2.0 / (images * ch)))[0:1, :]
    rank = up.shape[0]
    tail_rows = ua.shape[0] - rank
    ua[0:rank, :] = acc[0:rank, :] * factor
    a_top, a_rest = halves(jnp.concatenate([acc[rank : rank + ch, :], csum[...]], 0))
    tail = mm_nt(a_top, up) + mm_nt(a_rest, up)
    lower = jnp.concatenate([tail[0 : ch // 2], tail[ch // 2 : ch]], 1)
    lowest = jnp.concatenate([tail[ch:], tail[ch:]], 1)
    ua[rank:, :] = jnp.concatenate([lower, lowest], 0) * factor

    def to(r):
        return {"pair": lax.div(r, dps), "dp": lax.rem(r, dps)}

    def u_copy(owner, peer):
        return remote(
            ua.at[pl.ds(0, rank)], ubuf.at[owner], u_s.at[peer], u_r.at[owner], to(peer)
        )

    def a_copy(owner, peer):
        return remote(
            ua.at[pl.ds(rank, tail_rows)],
            abuf.at[owner],
            a_s.at[peer],
            a_r.at[owner],
            {"seq": peer},
        )

    def v_copy(owner, peer):
        return remote(
            usum,
            upb.at[:, at_lanes(owner * 128, 128)],
            v_s.at[peer],
            v_r.at[owner],
            {"seq": peer},
        )

    def b_copy(owner, peer):
        return remote(asum, a2.at[owner], b_s.at[peer], b_r.at[owner], to(peer))

    others(rep, reps, lambda peer: u_copy(rep, peer).start())
    others(me, seqs, lambda peer: a_copy(me, peer).start())
    ubuf[rep] = ua[0:rank, :]
    abuf[me] = ua[rank:, :]

    others(rep, reps, lambda peer: u_copy(peer, peer).wait_recv())
    sums = jnp.sum(ubuf[...], 0).astype(BF16)
    usum[...] = sums
    upb[:, at_lanes(me * 128, 128)] = sums
    others(me, seqs, lambda peer: v_copy(me, peer).start())
    others(me, seqs, lambda peer: a_copy(peer, peer).wait_recv())
    sums = jnp.sum(abuf[...], 0)
    asum[...] = sums
    a2[rep] = sums
    others(rep, reps, lambda peer: b_copy(rep, peer).start())

    def sent(peer):
        mod_copy(me, peer).wait_send()
        noisy_copy(me, peer).wait_send()
        for kind in range(2):
            out_copy(kind, me, peer).wait_send()
        gap_copy(slot, slot, me, peer).wait_send()
        gap_copy(other, slot, me, peer).wait_send()
        g_copy(me, peer).wait_send()
        a_copy(me, peer).wait_send()

    others(me, seqs, sent)
    gap_copy(other, slot, me, me).wait_send()
    for kind in range(2):
        ring_sent(kind)
    for copy in kv_copies(slot):
        copy.wait_send()
    if origins > 1:
        for way in range(2):
            for turn in range(2):
                x_near(way, turn, mine).wait_send()
            x_far(way, mine).wait_send()
    for which in range(origins):
        for side in range(2):
            y_copy(which, side, slot).wait_send()
            c_copy(0, which, side, False).wait_send()
            c_copy(1, which, side, False).wait_send()

    others(rep, reps, lambda peer: b_copy(peer, peer).wait_recv())
    for p in range(dps):
        a = a2[p] + a2[dps + p]
        top = a[0 : ch // 2]
        low_rows = a[ch // 2 :, 0:ch]
        right[p * deep : (p + 1) * deep, :] = jnp.concatenate(
            [top[:, 0:ch], top[:, ch:], low_rows, low_rows], 0
        ).astype(BF16)
    down[...] = mm_tn(right[...], left[...]).astype(BF16)

    def last_sent(peer):
        v_copy(me, peer).wait_send()
        v_copy(peer, peer).wait_recv()

    others(me, seqs, last_sent)

    def last_reps(peer):
        u_copy(rep, peer).wait_send()
        b_copy(rep, peer).wait_send()

    others(rep, reps, last_reps)


def shape(dims, kind):
    return jax.ShapeDtypeStruct(dims, kind)


def on_device(
    latents,
    noise,
    pair_timestep_index,
    preferred_image_slot,
    prompt_token_states,
    image_embed_weight,
    timestep_modulation_weight,
    image_query_key_value,
    text_key_value,
    query_norm_gain,
    key_norm_gain,
    adapter_down_weight,
    adapter_up_weight,
    image_output_weight,
    latent_out_weight,
):
    seqs = lax.axis_size("seq")
    dps = lax.axis_size("dp")
    rows, ch = latents.shape[2:]
    images = rows * seqs
    width = image_embed_weight.shape[1]
    texts = prompt_token_states.shape[1] * seqs
    keys = images + texts
    rank = adapter_down_weight.shape[1]
    step_value = pair_timestep_index[0].astype(jnp.float32)
    emb = sinusoid(step_value, timestep_modulation_weight.shape[0]).astype(BF16)[None]
    V, S, A = pltpu.VMEM, pltpu.SMEM, pl.ANY
    DMA = pltpu.SemaphoreType.DMA
    heads = 128 * seqs
    tail = ch // 2 + 8
    deep = ch + 16
    reps = 2 * dps
    scratch = [
        V((width, 384), BF16),
        V((width, 256), BF16),
        V((1, 6 * width), F32),
        V((dps, 1, 2 * width), F32),
        V((seqs, rows // 2, 128), BF16),
        V((texts // 2, width), BF16),
        V((2 * images, 256), F32),
        V((2 * images, 128), BF16),
        V((2 * images, 128), BF16),
        V((1, timestep_modulation_weight.shape[1]), F32),
        V((2 * rows, heads), BF16),
        V((seqs, 128, width), BF16),
        V((keys, 128), BF16),
        V((keys, 256), BF16),
        V((images, 128), F32),
        V((images, 128), BF16),
        V((images, 128), F32),
        V((images, 128), F32),
        V((2 * rows, width), F32),
        V((rows, width), BF16),
        V((images, 128), BF16),
        V((seqs, rows, 128), BF16),
        V((2 * seqs, 8, 128), F32),
        V((rank + ch, 128), F32),
        V((8, 128), F32),
        V((rank + tail, 128), F32),
        V((reps, rank, 128), F32),
        V((seqs, tail, 128), F32),
        V((reps, tail, 128), F32),
        V((rank, 128), BF16),
        V((tail, 128), F32),
        V((dps * deep, width), BF16),
        V((dps * deep, ch), BF16),
    ]
    one = DMA((seqs,))
    ring = [DMA((3 * seqs,)), one]
    scratch += [DMA((3,))] + [one] * 4 + ring + [DMA((dps,))] * 2 + [DMA((2,))] * 2
    scratch += [DMA((2, seqs))] * 2 + [one] * 2 + [DMA((2 * seqs,))] * 2 + ring
    scratch += [DMA((6,))] * 2 + [DMA((8,))] * 2 + [DMA((16,))] * 2
    scratch += [DMA((reps,))] * 2 + [one] * 4 + [DMA((reps,))] * 2
    down_t, up, value = pl.pallas_call(
        functools.partial(main_kernel, seqs, dps),
        out_shape=[shape((ch, width), BF16), shape((rank, heads), BF16), shape((1, 1), F32)],
        in_specs=[
            pl.BlockSpec(memory_space=m)
            for m in [S, S, V, V, V, V, V, V, A, A, V, V, V, V, A, V]
        ],
        out_specs=[pl.BlockSpec(memory_space=V)] * 3,
        scratch_shapes=scratch,
        compiler_params=pltpu.CompilerParams(
            collective_id=0, has_side_effects=True, vmem_limit_bytes=VMEM_BYTES
        ),
    )(
        pair_timestep_index,
        preferred_image_slot,
        emb,
        latents[0, 0].T,
        noise[0].T,
        prompt_token_states[0],
        image_embed_weight,
        timestep_modulation_weight,
        image_query_key_value.reshape(width, -1),
        text_key_value.reshape(width, -1),
        query_norm_gain.reshape(1, -1),
        key_norm_gain.reshape(1, -1),
        adapter_down_weight.T,
        adapter_up_weight,
        image_output_weight,
        latent_out_weight.T,
    )
    return (down_t.T.astype(F32), up.astype(F32), value.reshape(1))


def solution(mesh):
    return jax.shard_map(
        on_device,
        mesh=mesh,
        in_specs=(
            P("dp", "pair", "seq", None),
            P("dp", "seq", None),
            P("dp"),
            P("dp"),
            P("dp", "seq", None),
            P(),
            P(None, "seq"),
            P(None, "seq", None),
            P(None, "seq", None),
            P(),
            P(),
            P(),
            P(),
            P("seq", None),
            P(),
        ),
        out_specs=(P(), P(), P("dp")),
        check_vma=False,
    )
```

time: 178 us -> 146 us (0.82)
  Pallas kernels: 167 us -> 138 us
  local copies, waits for them, and re-layouts: 8.56 us -> 0 us
  other arithmetic: 0.06 us -> 4.33 us
    pallas_call x2 -> x1, Pallas kernels: 167 us -> 138 us  [on_device(): pl.pallas_call(functools.partial(main_kernel, seqs, dps), out_shape=[shap...]
    unnamed x4 -> x0, local copies, waits for them, and re-layouts: 6.78 us -> none
    convert_element_type x0 -> x2, other arithmetic: none -> 3.7 us  [on_device(): return (down_t.T.astype(F32), up.astype(F32), value.reshape(1))]
where the time goes in v3:
time: 146 us
  Pallas kernels  138 us (95%)
  other arithmetic  4.33 us (3%)
  between operations  3.7 us (3%)
    pallas_call x1, Pallas kernels, on_device(): pl.pallas_call(functools.partial(main_kernel, seqs, dps), out_shape=[shap...  138 us
    convert_element_type x2, other arithmetic, on_device(): return (down_t.T.astype(F32), up.astype(F32), value.reshape(1))  3.7 us

profile of v3, /device:TPU:1, one launch (start us, length us, event | category | flops | bytes accessed | tf_op | source)
XLA Modules:
  0.0 145.5 jit_solution(7839479934801219891)
XLA Ops:
  1.9 0.1 convert_bitcast_fusion.1
  2.0 0.6 pad_maximum_fusion.emb
  2.6 137.5 %shard_map.166 = (bf16[64,3072]{1,0:T(8,128)(2,1)}, bf16[64,2048]{1,0:T(8,128)(2,1)}, f32[1,1]{1,0:T(1,128)}) custom-call(s32[1]{0:T(128)S(6)} %copy.19.step, s32[1]{0:T(128)S(6)} %copy.20.pref, bf16[1,256]{1,0:T(2,128)(2,1)} %pad_maximum_fusion.emb, bf16[64,96]{1,0:T(8,128)(2,1)} %bitcast.26, bf16[64,96]{1,0:T(8,128)(2,1)} %bitcast.27, ...), custom_call_target="tpu_custom_call" | custom-call | tf_op jit(solution)/shard_map/pallas_call | solution.py:815
  140.1 1.9 %convert_bitcast_fusion = f32[3072,64]{0,1:T(8,128)} fusion(bf16[64,3072]{1,0:T(8,128)(2,1)} %get-tuple-element.6), kind=kLoop, calls=%fused_computation | loop fusion | flops 196608 | bytes 1179648 | tf_op jit(solution)/shard_map/convert_element_type | solution.py:845
  142.0 1.8 %convert_element_type.27 = f32[64,2048]{1,0:T(8,128)} convert(bf16[64,2048]{1,0:T(8,128)(2,1)} %get-tuple-element.7) | non-fusion elementwise | flops 131072 | bytes 786432 | tf_op jit(solution)/shard_map/convert_element_type | solution.py:845

commit v4 on v3

--- a/solution.py
+++ b/solution.py
@@ -76,22 +76,12 @@
         body(lax.rem(me + step, count))
 
 
-def greet(axes):
-    barrier = pltpu.get_barrier_semaphore()
-    total = 0
-    for axis, me, count in axes:
-        others(
-            me,
-            count,
-            lambda peer: pl.semaphore_signal(
-                barrier,
-                inc=1,
-                device_id={axis: peer},
-                device_id_type=pl.DeviceIdType.MESH,
-            ),
-        )
-        total += count - 1
-    return barrier, total
+def arrived(ref, sem, device):
+    remote(ref, ref, sem, sem, device).wait_recv()
+
+
+def gone(ref, sem, device):
+    remote(ref, ref, sem, sem, device).wait_send()
 
 
 def at_rows(start, size):
@@ -117,7 +107,7 @@
 def main_kernel(
     seqs, dps, step, pref, emb, lat_t, noi_t, txt, embed, wmod, wimg, wtxt, qg, kg, adown_t, aup, wo, lw_t,
     down, upb, value,
-    wimg_v, wtxt_v, mod, moddp, noisy, text, oacc, q2, outb, modrow, x, wall, kk, vext, pol, lhs, outf, rl,
+    wimg_v, wtxt_v, adown_v, up_v, lw_v, mod, moddp, noisy, text, oacc, q2, outb, modrow, x, wall, kk, vext, pol, lhs, outf, rl,
     mixed, gmix, gh, ghs, gapbuf, acc, csum, ua, ubuf, abuf, a2, usum, asum, left, right,
     in_s, mod_s, mod_r, noi_s, noi_r, txt_s, txt_r, dp_s, dp_r, kv_s, kv_r, x_s, x_r,
     g_s, g_r, e_s, e_r, wz_s, wz_r, wx_s, wx_r, wy_s, wy_r, wc_s, wc_r,
@@ -152,19 +142,27 @@
         ),
         pltpu.make_async_copy(wimg, wimg_v, in_s.at[1]),
         pltpu.make_async_copy(wtxt, wtxt_v, in_s.at[2]),
+        pltpu.make_async_copy(adown_t, adown_v, in_s.at[3]),
+        pltpu.make_async_copy(aup.at[:, at_lanes(me * 128, 128)], up_v, in_s.at[4]),
+        pltpu.make_async_copy(lw_t, lw_v, in_s.at[5]),
     ]
     for load in loads:
         load.start()
-    barrier, total = greet([("seq", me, seqs), ("dp", mine, dps)])
-    total += seqs + dps - 1
-
-    def greet_other(device):
+    barrier = pltpu.get_barrier_semaphore()
+
+    def at(seq=me, pair=slot, dp=mine):
+        return {"pair": pair, "seq": seq, "dp": dp}
+
+    def greet(device):
         pl.semaphore_signal(
             barrier, inc=1, device_id=device, device_id_type=pl.DeviceIdType.MESH
         )
 
-    each(seqs, lambda peer: greet_other({"seq": peer, "pair": other}))
-    others(mine, dps, lambda peer: greet_other({"dp": peer, "pair": other}))
+    others(me, seqs, lambda peer: greet(at(seq=peer)))
+    others(mine, dps, lambda peer: greet(at(dp=peer)))
+    each(dps, lambda peer: greet(at(pair=other, dp=peer)))
+    greet(at(seq=flip, pair=other))
+    total = (seqs - 1) + (dps - 1) + dps + 1
 
     mod_part = mm(jnp.broadcast_to(emb[...].astype(F32), (16, emb.shape[1])).astype(BF16), wmod[...])[0:1]
     modrow[...] = mod_part
@@ -177,6 +175,13 @@
     t = txt[at_rows(slot * half, half), :].astype(F32)
     t = t - row_mean(t)
     text[at_rows(me * half, half), :] = (t * lax.rsqrt(row_mean(t * t) + epsilon)).astype(BF16)
+    emb_c = embed[...].astype(F32)
+    emb_c = emb_c - row_mean(emb_c)
+    e_top, e_rest = halves(emb_c)
+    gram = stacked(mm_nt(e_top, e_top) + mm_nt(e_top, e_rest) + mm_nt(e_rest, e_top))
+    vext[:, 128:256] = jnp.ones((vext.shape[0], 128), BF16)
+    acc[...] = jnp.zeros_like(acc)
+    csum[...] = jnp.zeros_like(csum)
     loads[0].wait()
     pl.semaphore_wait(barrier, total)
 
@@ -184,22 +189,22 @@
         return remote(
             modrow,
             mod.at[:, at_lanes(owner * part, part)],
-            mod_s.at[peer],
-            mod_r.at[owner],
-            {"seq": peer},
+            mod_s.at[0],
+            mod_r.at[0],
+            at(seq=peer),
         )
 
     def noisy_copy(owner, peer):
         where = noisy.at[owner]
-        return remote(where, where, noi_s.at[peer], noi_r.at[owner], {"seq": peer})
+        return remote(where, where, noi_s.at[0], noi_r.at[0], at(seq=peer))
 
     def dp_copy(owner, peer):
         return remote(
             mod.at[:, pl.ds(0, 2 * width)],
             moddp.at[owner],
-            dp_s.at[peer],
-            dp_r.at[owner],
-            {"dp": peer},
+            dp_s.at[0],
+            dp_r.at[0],
+            at(dp=peer),
         )
 
     def region(first, count, p, s):
@@ -215,7 +220,7 @@
             where, send, recv = region(owner, 1, mine, slot), wz_s, wz_r
         else:
             where, send, recv = text.at[at_rows(owner * half, half)], txt_s, txt_r
-        return remote(where, where, send.at[lane * seqs + owner], recv.at[owner], {"seq": to})
+        return remote(where, where, send.at[lane * seqs + owner], recv.at[owner], at(seq=to))
 
     def ring_sends(kind, hop):
         last = hop == zs // 2
@@ -270,26 +275,26 @@
 
     def x_near(way, turn, origin):
         where = chunk(origin, turn if way == 0 else 1 - turn, slot)
-        at = way * 2 + turn
-        return remote(where, where, wx_s.at[at], wx_r.at[at], {"dp": along(1 - 2 * way)})
+        n = way * 2 + turn
+        return remote(where, where, wx_s.at[n], wx_r.at[n], at(dp=along(1 - 2 * way)))
 
     def x_far(way, origin):
         where = chunk(origin, way, slot)
-        return remote(where, where, wx_s.at[4 + way], wx_r.at[4 + way], {"dp": along(1 - 2 * way)})
+        return remote(where, where, wx_s.at[4 + way], wx_r.at[4 + way], at(dp=along(1 - 2 * way)))
 
     def y_copy(which, side, s):
         where = chunk(places[which], side, s)
         to = me if side == 0 else flip
-        at = which * 2 + side
-        return remote(where, where, wy_s.at[at], wy_r.at[at], {"pair": other, "seq": to})
+        n = which * 2 + side
+        return remote(where, where, wy_s.at[n], wy_r.at[n], at(pair=other, seq=to))
 
     def c_copy(foreign, which, side, at_sibling):
         origin = places[which]
         if at_sibling:
             origin = sibling - mine + origin
         where = chunk(origin, side, other if foreign else slot)
-        at = (foreign * 4 + which) * 2 + side
-        return remote(where, where, wc_s.at[at], wc_r.at[at], {"dp": sibling})
+        n = (foreign * 4 + which) * 2 + side
+        return remote(where, where, wc_s.at[n], wc_r.at[n], at(dp=sibling))
 
     def spread(which, side):
         y_copy(which, side, slot).start()
@@ -307,14 +312,11 @@
     others(me, seqs, send_small)
     ring_first(0)
     mod[:, at_lanes(me * part, part)] = mod_part
-
-    emb_c = embed[...].astype(F32)
-    emb_c = emb_c - row_mean(emb_c)
-    e_top, e_rest = halves(emb_c)
-    gram = stacked(mm_nt(e_top, e_top) + mm_nt(e_top, e_rest) + mm_nt(e_rest, e_top))
     ring_hop(0, 1)
-
-    others(me, seqs, lambda peer: mod_copy(peer, peer).wait_recv())
+    ring_first(1)
+
+    mod_others = mod.at[:, pl.ds(0, (seqs - 1) * part)]
+    arrived(mod_others, mod_r.at[0], at(seq=flip))
     shift_img, scale_img, shift_txt, scale_txt, shift_out, scale_out = [
         mod[:, i * width : (i + 1) * width] for i in range(6)
     ]
@@ -324,22 +326,24 @@
         ring_hop(0, 2)
 
     loads[1].wait()
+    loads[3].wait()
+    loads[4].wait()
     img_lhs = with_shift(emb_c * (1.0 + scale_img), shift_img)
     img_m = mm(img_lhs, wimg_v[...])
     img_m2 = stacked(img_m[0:ch])
     img_shift = img_m[ch : ch + 1] + img_m[ch + 1 : ch + 2]
-    low_m = mm_nt(img_lhs, adown_t[...])
+    low_m = mm_nt(img_lhs, adown_v[...])
     low_m2 = stacked(low_m[0:ch])
     low_shift = low_m[ch : ch + 1] + low_m[ch + 1 : ch + 2]
-    up = aup[:, at_lanes(me * 128, 128)]
+    up = up_v[...]
     gain_q = qg[...]
     gain_k = kg[...]
     score_scale = math.log2(math.e) / math.sqrt(128.0)
-    vext[:, 128:256] = jnp.ones((vext.shape[0], 128), BF16)
     if hops > 2:
         ring_hop(0, 3)
 
-    others(me, seqs, lambda peer: noisy_copy(peer, peer).wait_recv())
+    noisy_others = noisy.at[pl.ds(0, seqs - 1)]
+    arrived(noisy_others, noi_r.at[0], at(seq=flip))
 
     def project(i):
         here = at_rows(i * block, block)
@@ -375,7 +379,7 @@
     spans(0, blocks // 2, project)
     if hops > 3:
         ring_hop(0, 4)
-    ring_first(1)
+    ring_hop(1, 1)
     spans(blocks // 2, blocks, project)
     ring_end(0)
     if origins > 1:
@@ -384,7 +388,8 @@
                 x_near(way, turn, mine).start()
     spread(0, 0)
     spread(0, 1)
-    ring_hop(1, 1)
+    if hops > 1:
+        ring_hop(1, 2)
 
     def attend(here, keys):
         s = mm_nt(q2[here, :], kk[keys, :])
@@ -394,10 +399,9 @@
         here = at_rows(i * block, block)
         oacc[here, :] = attend(here, pl.ds(0, images))
 
-    spans(0, blocks // 2, image_keys)
-    if hops > 1:
-        ring_hop(1, 2)
-    spans(blocks // 2, blocks, image_keys)
+    spans(0, blocks, image_keys)
+    if hops > 2:
+        ring_hop(1, 3)
     if origins > 1:
         x_near(0, 0, places[1]).wait_recv()
         x_far(0, places[1]).start()
@@ -405,12 +409,10 @@
         x_near(1, 0, places[2]).wait_recv()
         x_far(1, places[2]).start()
         spread(2, 1)
-    if hops > 2:
-        ring_hop(1, 3)
     spans(blocks, 2 * blocks, image_keys)
-    relay(0)
     if hops > 3:
         ring_hop(1, 4)
+    relay(0)
     if origins > 1:
         x_near(0, 1, places[1]).wait_recv()
         spread(1, 1)
@@ -430,12 +432,18 @@
         keys = at_rows(images + owner * texts, texts)
         v = vext.at[keys, pl.ds(0, 128)]
         return (
-            remote(kk.at[keys], kk.at[keys], kv_s.at[0], kv_r.at[0], {"pair": other}),
-            remote(v, v, kv_s.at[1], kv_r.at[1], {"pair": other}),
+            remote(kk.at[keys], kk.at[keys], kv_s.at[0], kv_r.at[0], at(pair=other)),
+            remote(v, v, kv_s.at[1], kv_r.at[1], at(pair=other)),
         )
 
     for copy in kv_copies(slot):
         copy.start()
+
+    def own_text(i):
+        here = at_rows(i * block, block)
+        oacc[here, :] += attend(here, my_keys)
+
+    spans(0, blocks, own_text)
     for copy in kv_copies(other):
         copy.wait_recv()
 
@@ -443,22 +451,21 @@
         return remote(
             outb.at[at_rows(kind * images + peer * rows, rows)],
             x.at[at_rows(kind * rows, rows), at_lanes(owner * 128, 128)],
-            x_s.at[kind, peer],
-            x_r.at[kind, owner],
-            {"seq": peer},
-        )
-
-    def text_keys(i):
-        kind = lax.div(i, blocks)
+            x_s.at[kind],
+            x_r.at[kind],
+            at(seq=peer),
+        )
+
+    def text_keys(kind, i):
         b = lax.rem(i + lax.div(me, 4), blocks)
         here = at_rows(kind * images + b * block, block)
-        o = oacc[here, :] + attend(here, pl.ds(images, 2 * texts))
+        left_keys = at_rows(images + other * texts, texts) if kind == 0 else pl.ds(images, 2 * texts)
+        o = oacc[here, :] + attend(here, left_keys)
         inv = 1.0 / o[:, 128:256]
         out = o[:, 0:128] * inv
         outb[here, :] = out.astype(BF16)
 
-        @pl.when(kind == 1)
-        def _():
+        if kind == 1:
             outf[at_rows(b * block, block), :] = out
             rl[at_rows(b * block, block), :] = inv
 
@@ -475,7 +482,8 @@
                     at_rows(kind * images + me * rows, rows), :
                 ]
 
-    spans(0, 2 * blocks, text_keys)
+    for kind in range(2):
+        spans(0, blocks, functools.partial(text_keys, kind))
 
     if origins > 1:
         x_far(0, places[3]).wait_recv()
@@ -485,11 +493,8 @@
         relay(1)
         relay(2)
 
-    def finish_dp(peer):
-        dp_copy(mine, peer).wait_send()
-        dp_copy(peer, peer).wait_recv()
-
-    others(mine, dps, finish_dp)
+    moddp_others = moddp.at[pl.ds(0, dps - 1)]
+    arrived(moddp_others, dp_r.at[0], at(dp=sibling))
     first = lax.broadcasted_iota(jnp.int32, (16, width), 0) == 0
     deep = ch + 16
 
@@ -503,52 +508,48 @@
 
     for p in range(dps):
         build(p)
-    acc[...] = jnp.zeros_like(acc)
-    csum[...] = jnp.zeros_like(csum)
     if origins > 1:
         relay(3)
 
-    def finish_out(peer):
-        for kind in range(2):
-            out_copy(kind, peer, peer).wait_recv()
-
-    others(me, seqs, finish_out)
-    for which in range(origins):
-        for side in range(2):
-            c_copy(0, which, side, True).wait_recv()
-            c_copy(1, which, side, True).wait_recv()
-
-    tile = 256
+    out_others = [
+        x.at[pl.ds(kind * rows, rows), pl.ds(0, 128 * (seqs - 1))] for kind in range(2)
+    ]
+    for kind in range(2):
+        arrived(out_others[kind], x_r.at[kind], at(seq=flip))
+
+    loads[5].wait()
+    tile = 256 if span % 256 == 0 else 128
     xv = x[...]
 
-    def mix(i):
-        here = at_lanes(i * tile, tile)
+    def mix(i, first_lane):
+        here = at_lanes(first_lane + i * tile, tile)
         states = mm(own, embed[:, here])
         w = wall[:, :, here].reshape(128 * seqs, tile)
         mixed[:, here] = mm(xv, w) + jnp.concatenate([states, states], 0)
 
-    each(width // tile, mix)
+    for foreign in range(2):
+        for which in range(origins):
+            for side in range(2):
+                c_copy(foreign, which, side, True).wait_recv()
+        first_lane = (other if foreign else slot) * span
+        each(span // tile, lambda i: mix(i, first_lane))
     full = mixed[...]
     full = full - row_mean(full)
     inv = lax.rsqrt(row_mean(full * full) + epsilon)
     unit = full * inv
     mixed[...] = unit
-    pred = mm_nt((unit * (1.0 + scale_out) + shift_out).astype(BF16), lw_t[...])
+    pred = mm_nt((unit * (1.0 + scale_out) + shift_out).astype(BF16), lw_v[...])
     diff = jnp.concatenate([target, target], 0) - pred
     squares = diff * diff
     gap = (jnp.sum(squares[rows:]) - jnp.sum(squares[:rows])) * (1.0 / (images * ch))
-    gapbuf[slot * seqs + me] = jnp.full((8, 128), gap, F32)
-
-    def gap_copy(to_slot, from_slot, owner, peer):
+    gapbuf[me] = jnp.full((8, 128), gap, F32)
+
+    def gap_copy(owner, peer):
         return remote(
-            gapbuf.at[slot * seqs + me],
-            gapbuf.at[from_slot * seqs + owner],
-            e_s.at[to_slot * seqs + peer],
-            e_r.at[from_slot * seqs + owner],
-            {"seq": peer, "pair": to_slot},
-        )
-
-    g_ln = mm(diff[rows:].astype(BF16), lw_t[...]) * (1.0 + scale_out)
+            gapbuf.at[owner], gapbuf.at[owner], e_s.at[0], e_r.at[0], at(seq=peer)
+        )
+
+    g_ln = mm(diff[rows:].astype(BF16), lw_v[...]) * (1.0 + scale_out)
     unit_p = mixed[rows:, :]
     gmix[...] = (
         (g_ln - row_mean(g_ln) - unit_p * row_mean(g_ln * unit_p)) * inv[rows:]
@@ -558,9 +559,9 @@
         return remote(
             ghs.at[peer],
             gh.at[at_rows(owner * rows, rows)],
-            g_s.at[peer],
-            g_r.at[owner],
-            {"seq": peer},
+            g_s.at[0],
+            g_r.at[lax.div(owner, 4)],
+            at(seq=peer),
         )
 
     def heads_back(i):
@@ -581,25 +582,22 @@
 
     each(seqs // 2, heads_back)
 
-    def send_gap(peer):
-        gap_copy(slot, slot, me, peer).start()
-        gap_copy(other, slot, me, peer).start()
-
-    others(me, seqs, send_gap)
-    gap_copy(other, slot, me, me).start()
+    others(me, seqs, lambda peer: gap_copy(me, peer).start())
     keys = kk[...]
     vals = vext[:, 0:128]
 
     def back(i):
         b = lax.rem(i + lax.div(me, 4), blocks)
-        for j in range(4):
-            peer = b * 4 + j
-
-            @pl.when(peer != me)
-            def _():
-                g_copy(peer, peer).wait_recv()
-
         here = at_rows(b * block, block)
+
+        @pl.when(i == 0)
+        def _():
+            arrived(gh.at[pl.ds(0, 3 * rows)], g_r.at[b], at(seq=flip))
+
+        @pl.when(i != 0)
+        def _():
+            arrived(gh.at[pl.ds(0, 4 * rows)], g_r.at[b], at(seq=flip))
+
         g = gh[here, :]
         p = jnp.exp2(mm_nt(q2[at_rows(images + b * block, block), :], keys))
         gp = mm_nt(g, vals)
@@ -615,16 +613,18 @@
             jnp.sum(gd.astype(F32), 0, keepdims=True), csum.shape
         )
 
-    each(blocks, back)
-
-    def wait_gap(peer):
-        gap_copy(slot, slot, peer, peer).wait_recv()
-        gap_copy(slot, other, peer, peer).wait_recv()
-
-    others(me, seqs, wait_gap)
-    gap_copy(slot, other, me, me).wait_recv()
-    own_gap = jnp.sum(gapbuf[pl.ds(slot * seqs, seqs)], 0)
-    other_gap = jnp.sum(gapbuf[pl.ds(other * seqs, seqs)], 0)
+    gap_others = gapbuf.at[pl.ds(0, seqs - 1)]
+    pair_copy = remote(
+        gapbuf.at[seqs], gapbuf.at[seqs + 1], e_s.at[1], e_r.at[1], at(pair=other)
+    )
+    spans(0, blocks // 2, back)
+    arrived(gap_others, e_r.at[0], at(seq=flip))
+    own_gap = jnp.sum(gapbuf[0:seqs], 0)
+    gapbuf[seqs] = own_gap
+    pair_copy.start()
+    spans(blocks // 2, blocks, back)
+    pair_copy.wait_recv()
+    other_gap = gapbuf[seqs + 1]
     sgn = (1.0 - 2.0 * pref[0].astype(F32)) * (1.0 - 2.0 * slot.astype(F32))
     z = half_beta * sgn * (own_gap - other_gap)
     value[...] = (jnp.maximum(z, 0.0) + jnp.log1p(jnp.exp(-jnp.abs(z))))[0:1, 0:1]
@@ -640,62 +640,61 @@
     ua[rank:, :] = jnp.concatenate([lower, lowest], 0) * factor
 
     def to(r):
-        return {"pair": lax.div(r, dps), "dp": lax.rem(r, dps)}
+        return at(pair=lax.div(r, dps), dp=lax.rem(r, dps))
 
     def u_copy(owner, peer):
         return remote(
-            ua.at[pl.ds(0, rank)], ubuf.at[owner], u_s.at[peer], u_r.at[owner], to(peer)
+            ua.at[pl.ds(0, rank)], ubuf.at[owner], u_s.at[0], u_r.at[0], to(peer)
         )
 
     def a_copy(owner, peer):
         return remote(
             ua.at[pl.ds(rank, tail_rows)],
             abuf.at[owner],
-            a_s.at[peer],
-            a_r.at[owner],
-            {"seq": peer},
+            a_s.at[0],
+            a_r.at[0],
+            at(seq=peer),
         )
 
     def v_copy(owner, peer):
         return remote(
             usum,
             upb.at[:, at_lanes(owner * 128, 128)],
-            v_s.at[peer],
-            v_r.at[owner],
-            {"seq": peer},
+            v_s.at[0],
+            v_r.at[0],
+            at(seq=peer),
         )
 
     def b_copy(owner, peer):
-        return remote(asum, a2.at[owner], b_s.at[peer], b_r.at[owner], to(peer))
-
+        return remote(asum, a2.at[owner], b_s.at[0], b_r.at[0], to(peer))
+
+    others(me, seqs, lambda peer: a_copy(me, peer).start())
     others(rep, reps, lambda peer: u_copy(rep, peer).start())
-    others(me, seqs, lambda peer: a_copy(me, peer).start())
     ubuf[rep] = ua[0:rank, :]
     abuf[me] = ua[rank:, :]
 
-    others(rep, reps, lambda peer: u_copy(peer, peer).wait_recv())
+    u_others, a_others = ubuf.at[pl.ds(0, reps - 1)], abuf.at[pl.ds(0, seqs - 1)]
+    arrived(u_others, u_r.at[0], at(dp=sibling))
     sums = jnp.sum(ubuf[...], 0).astype(BF16)
     usum[...] = sums
     upb[:, at_lanes(me * 128, 128)] = sums
     others(me, seqs, lambda peer: v_copy(me, peer).start())
-    others(me, seqs, lambda peer: a_copy(peer, peer).wait_recv())
+    arrived(a_others, a_r.at[0], at(seq=flip))
     sums = jnp.sum(abuf[...], 0)
     asum[...] = sums
     a2[rep] = sums
     others(rep, reps, lambda peer: b_copy(rep, peer).start())
 
-    def sent(peer):
-        mod_copy(me, peer).wait_send()
-        noisy_copy(me, peer).wait_send()
-        for kind in range(2):
-            out_copy(kind, me, peer).wait_send()
-        gap_copy(slot, slot, me, peer).wait_send()
-        gap_copy(other, slot, me, peer).wait_send()
-        g_copy(me, peer).wait_send()
-        a_copy(me, peer).wait_send()
-
-    others(me, seqs, sent)
-    gap_copy(other, slot, me, me).wait_send()
+    near = at(seq=flip)
+    gone(mod_others, mod_s.at[0], near)
+    gone(noisy_others, noi_s.at[0], near)
+    gone(moddp_others, dp_s.at[0], near)
+    for kind in range(2):
+        gone(out_others[kind], x_s.at[kind], near)
+    gone(gh.at[pl.ds(0, (seqs - 1) * rows)], g_s.at[0], near)
+    gone(gap_others, e_s.at[0], near)
+    pair_copy.wait_send()
+    gone(a_others, a_s.at[0], near)
     for kind in range(2):
         ring_sent(kind)
     for copy in kv_copies(slot):
@@ -711,7 +710,8 @@
             c_copy(0, which, side, False).wait_send()
             c_copy(1, which, side, False).wait_send()
 
-    others(rep, reps, lambda peer: b_copy(peer, peer).wait_recv())
+    b_others = a2.at[pl.ds(0, reps - 1)]
+    arrived(b_others, b_r.at[0], near)
     for p in range(dps):
         a = a2[p] + a2[dps + p]
         top = a[0 : ch // 2]
@@ -721,17 +721,11 @@
         ).astype(BF16)
     down[...] = mm_tn(right[...], left[...]).astype(BF16)
 
-    def last_sent(peer):
-        v_copy(me, peer).wait_send()
-        v_copy(peer, peer).wait_recv()
-
-    others(me, seqs, last_sent)
-
-    def last_reps(peer):
-        u_copy(rep, peer).wait_send()
-        b_copy(rep, peer).wait_send()
-
-    others(rep, reps, last_reps)
+    v_others = upb.at[:, pl.ds(0, 128 * (seqs - 1))]
+    gone(v_others, v_s.at[0], near)
+    arrived(v_others, v_r.at[0], near)
+    gone(u_others, u_s.at[0], near)
+    gone(b_others, b_s.at[0], near)
 
 
 def shape(dims, kind):
@@ -774,6 +768,9 @@
     scratch = [
         V((width, 384), BF16),
         V((width, 256), BF16),
+        V((rank, width), BF16),
+        V((rank, 128), BF16),
+        V((ch, width), BF16),
         V((1, 6 * width), F32),
         V((dps, 1, 2 * width), F32),
         V((seqs, rows // 2, 128), BF16),
@@ -794,7 +791,7 @@
         V((rows, width), BF16),
         V((images, 128), BF16),
         V((seqs, rows, 128), BF16),
-        V((2 * seqs, 8, 128), F32),
+        V((seqs + 2, 8, 128), F32),
         V((rank + ch, 128), F32),
         V((8, 128), F32),
         V((rank + tail, 128), F32),
@@ -806,18 +803,17 @@
         V((dps * deep, width), BF16),
         V((dps * deep, ch), BF16),
     ]
-    one = DMA((seqs,))
-    ring = [DMA((3 * seqs,)), one]
-    scratch += [DMA((3,))] + [one] * 4 + ring + [DMA((dps,))] * 2 + [DMA((2,))] * 2
-    scratch += [DMA((2, seqs))] * 2 + [one] * 2 + [DMA((2 * seqs,))] * 2 + ring
-    scratch += [DMA((6,))] * 2 + [DMA((8,))] * 2 + [DMA((16,))] * 2
-    scratch += [DMA((reps,))] * 2 + [one] * 4 + [DMA((reps,))] * 2
+    one = DMA((1,))
+    ring = [DMA((3 * seqs,)), DMA((seqs,))]
+    scratch += [DMA((6,))] + [one] * 4 + ring + [one] * 2 + [DMA((2,))] * 2
+    scratch += [DMA((2,))] * 2 + [one, DMA((seqs // 4,))] + [DMA((2,))] * 2 + ring
+    scratch += [DMA((6,))] * 2 + [DMA((8,))] * 2 + [DMA((16,))] * 2 + [one] * 8
     down_t, up, value = pl.pallas_call(
         functools.partial(main_kernel, seqs, dps),
         out_shape=[shape((ch, width), BF16), shape((rank, heads), BF16), shape((1, 1), F32)],
         in_specs=[
             pl.BlockSpec(memory_space=m)
-            for m in [S, S, V, V, V, V, V, V, A, A, V, V, V, V, A, V]
+            for m in [S, S, V, V, V, V, V, V, A, A, V, V, A, A, A, A]
         ],
         out_specs=[pl.BlockSpec(memory_space=V)] * 3,
         scratch_shapes=scratch,

time: 146 us -> 140 us (0.959)
  Pallas kernels: 138 us -> 131 us
    pallas_call x1, Pallas kernels: 138 us -> 131 us  [on_device(): pl.pallas_call(functools.partial(main_kernel, seqs, dps), out_shape=[shap...]
where the time goes in v4:
time: 140 us; the launch traced here: 139 us
  Pallas kernels  131 us (94%)
  other arithmetic  4.33 us (3%)
  between operations  3.7 us (3%)
    pallas_call x1, Pallas kernels, on_device(): pl.pallas_call(functools.partial(main_kernel, seqs, dps), out_shape=[shap...  131 us
    convert_element_type x2, other arithmetic, on_device(): return (down_t.T.astype(F32), up.astype(F32), value.reshape(1))  3.7 us

profile of v4, /device:TPU:1, one launch (start us, length us, event | category | flops | bytes accessed | tf_op | source)
XLA Modules:
  0.0 139.4 jit_solution(2793689030359295832)
XLA Ops:
  1.9 0.1 convert_bitcast_fusion.1
  2.0 0.6 pad_maximum_fusion.emb
  2.6 131.4 %shard_map.166 = (bf16[64,3072]{1,0:T(8,128)(2,1)}, bf16[64,2048]{1,0:T(8,128)(2,1)}, f32[1,1]{1,0:T(1,128)}) custom-call(s32[1]{0:T(128)S(6)} %copy.19.step, s32[1]{0:T(128)S(6)} %copy.20.pref, bf16[1,256]{1,0:T(2,128)(2,1)} %pad_maximum_fusion.emb, bf16[64,96]{1,0:T(8,128)(2,1)} %bitcast.26, bf16[64,96]{1,0:T(8,128)(2,1)} %bitcast.27, ...), custom_call_target="tpu_custom_call" | custom-call | tf_op jit(solution)/shard_map/pallas_call | solution.py:811
  133.9 1.9 %convert_bitcast_fusion = f32[3072,64]{0,1:T(8,128)} fusion(bf16[64,3072]{1,0:T(8,128)(2,1)} %get-tuple-element.6), kind=kLoop, calls=%fused_computation | loop fusion | flops 196608 | bytes 1179648 | tf_op jit(solution)/shard_map/convert_element_type | solution.py:841
  135.9 1.8 %convert_element_type.27 = f32[64,2048]{1,0:T(8,128)} convert(bf16[64,2048]{1,0:T(8,128)(2,1)} %get-tuple-element.7) | non-fusion elementwise | flops 131072 | bytes 786432 | tf_op jit(solution)/shard_map/convert_element_type | solution.py:841

commit v5 on v4

--- a/solution.py
+++ b/solution.py
@@ -232,8 +232,10 @@
                 sends.append(ring_copy(kind, 2, owner_at(h, hop - 1), left_z))
         return sends
 
+    def ring_flip(kind):
+        ring_copy(kind, 0, me, flip).start()
+
     def ring_first(kind):
-        ring_copy(kind, 0, me, flip).start()
         if zs > 2:
             ring_copy(kind, 1, me, right_z).start()
             ring_copy(kind, 2, me, left_z).start()
@@ -282,6 +284,10 @@
         where = chunk(origin, way, slot)
         return remote(where, where, wx_s.at[4 + way], wx_r.at[4 + way], at(dp=along(1 - 2 * way)))
 
+    def x_other(way, origin):
+        where = chunk(origin, way, other)
+        return remote(where, where, wx_s.at[6 + way], wx_r.at[6 + way], at(dp=along(1 - 2 * way)))
+
     def y_copy(which, side, s):
         where = chunk(places[which], side, s)
         to = me if side == 0 else flip
@@ -300,20 +306,17 @@
         y_copy(which, side, slot).start()
         c_copy(0, which, side, False).start()
 
-    def relay(which):
-        for side in range(2):
-            y_copy(which, side, other).wait_recv()
-            c_copy(1, which, side, False).start()
-
-    def send_small(peer):
-        mod_copy(me, peer).start()
-        noisy_copy(me, peer).start()
-
-    others(me, seqs, send_small)
+    def relay(which, side):
+        y_copy(which, side, other).wait_recv()
+        c_copy(1, which, side, False).start()
+
+    others(me, seqs, lambda peer: mod_copy(me, peer).start())
+    ring_flip(0)
     ring_first(0)
+    others(me, seqs, lambda peer: noisy_copy(me, peer).start())
+    ring_flip(1)
     mod[:, at_lanes(me * part, part)] = mod_part
     ring_hop(0, 1)
-    ring_first(1)
 
     mod_others = mod.at[:, pl.ds(0, (seqs - 1) * part)]
     arrived(mod_others, mod_r.at[0], at(seq=flip))
@@ -322,8 +325,6 @@
     ]
     moddp[mine] = mod[:, 0 : 2 * width]
     others(mine, dps, lambda peer: dp_copy(mine, peer).start())
-    if hops > 1:
-        ring_hop(0, 2)
 
     loads[1].wait()
     loads[3].wait()
@@ -339,8 +340,10 @@
     gain_q = qg[...]
     gain_k = kg[...]
     score_scale = math.log2(math.e) / math.sqrt(128.0)
-    if hops > 2:
-        ring_hop(0, 3)
+    if hops > 1:
+        ring_hop(0, 2)
+    ring_first(1)
+    ring_hop(1, 1)
 
     noisy_others = noisy.at[pl.ds(0, seqs - 1)]
     arrived(noisy_others, noi_r.at[0], at(seq=flip))
@@ -377,10 +380,24 @@
             body(i)
 
     spans(0, blocks // 2, project)
+    if hops > 2:
+        ring_hop(0, 3)
+    spans(blocks // 2, blocks, project)
     if hops > 3:
         ring_hop(0, 4)
-    ring_hop(1, 1)
-    spans(blocks // 2, blocks, project)
+
+    def attend(here, keys):
+        s = mm_nt(q2[here, :], kk[keys, :])
+        return mm(jnp.exp2(s).astype(BF16), vext[keys, :])
+
+    def image_keys(i):
+        here = at_rows(i * block, block)
+        oacc[here, :] = attend(here, pl.ds(0, images))
+
+    cuts = [min(cut, 2 * blocks) for cut in (0, 1, 4)] + [2 * blocks]
+    spans(cuts[0], cuts[1], image_keys)
+    if hops > 1:
+        ring_hop(1, 2)
     ring_end(0)
     if origins > 1:
         for turn in range(2):
@@ -388,20 +405,12 @@
                 x_near(way, turn, mine).start()
     spread(0, 0)
     spread(0, 1)
-    if hops > 1:
-        ring_hop(1, 2)
-
-    def attend(here, keys):
-        s = mm_nt(q2[here, :], kk[keys, :])
-        return mm(jnp.exp2(s).astype(BF16), vext[keys, :])
-
-    def image_keys(i):
-        here = at_rows(i * block, block)
-        oacc[here, :] = attend(here, pl.ds(0, images))
-
-    spans(0, blocks, image_keys)
+    spans(cuts[1], cuts[2], image_keys)
     if hops > 2:
         ring_hop(1, 3)
+    spans(cuts[2], cuts[3], image_keys)
+    if hops > 3:
+        ring_hop(1, 4)
     if origins > 1:
         x_near(0, 0, places[1]).wait_recv()
         x_far(0, places[1]).start()
@@ -409,15 +418,8 @@
         x_near(1, 0, places[2]).wait_recv()
         x_far(1, places[2]).start()
         spread(2, 1)
-    spans(blocks, 2 * blocks, image_keys)
-    if hops > 3:
-        ring_hop(1, 4)
-    relay(0)
-    if origins > 1:
-        x_near(0, 1, places[1]).wait_recv()
-        spread(1, 1)
-        x_near(1, 1, places[2]).wait_recv()
-        spread(2, 0)
+    relay(0, 0)
+    relay(0, 1)
 
     ring_end(1)
     loads[2].wait()
@@ -444,6 +446,11 @@
         oacc[here, :] += attend(here, my_keys)
 
     spans(0, blocks, own_text)
+    if origins > 1:
+        x_near(0, 1, places[1]).wait_recv()
+        spread(1, 1)
+        x_near(1, 1, places[2]).wait_recv()
+        spread(2, 0)
     for copy in kv_copies(other):
         copy.wait_recv()
 
@@ -486,12 +493,15 @@
         spans(0, blocks, functools.partial(text_keys, kind))
 
     if origins > 1:
-        x_far(0, places[3]).wait_recv()
-        spread(3, 0)
-        x_far(1, places[3]).wait_recv()
-        spread(3, 1)
-        relay(1)
-        relay(2)
+        relay(1, 0)
+        x_other(0, places[1]).start()
+        relay(2, 1)
+        x_other(1, places[2]).start()
+        for way in range(2):
+            x_far(way, places[3]).wait_recv()
+            c_copy(0, 3, way, False).start()
+        relay(1, 1)
+        relay(2, 0)
 
     moddp_others = moddp.at[pl.ds(0, dps - 1)]
     arrived(moddp_others, dp_r.at[0], at(dp=sibling))
@@ -509,7 +519,9 @@
     for p in range(dps):
         build(p)
     if origins > 1:
-        relay(3)
+        for way in range(2):
+            x_other(way, places[3]).wait_recv()
+            c_copy(1, 3, way, False).start()
 
     out_others = [
         x.at[pl.ds(kind * rows, rows), pl.ds(0, 128 * (seqs - 1))] for kind in range(2)
@@ -704,9 +716,11 @@
             for turn in range(2):
                 x_near(way, turn, mine).wait_send()
             x_far(way, mine).wait_send()
+            x_other(way, mine).wait_send()
     for which in range(origins):
         for side in range(2):
-            y_copy(which, side, slot).wait_send()
+            if which < 3:
+                y_copy(which, side, slot).wait_send()
             c_copy(0, which, side, False).wait_send()
             c_copy(1, which, side, False).wait_send()
 
@@ -807,7 +821,7 @@
     ring = [DMA((3 * seqs,)), DMA((seqs,))]
     scratch += [DMA((6,))] + [one] * 4 + ring + [one] * 2 + [DMA((2,))] * 2
     scratch += [DMA((2,))] * 2 + [one, DMA((seqs // 4,))] + [DMA((2,))] * 2 + ring
-    scratch += [DMA((6,))] * 2 + [DMA((8,))] * 2 + [DMA((16,))] * 2 + [one] * 8
+    scratch += [DMA((8,))] * 2 + [DMA((8,))] * 2 + [DMA((16,))] * 2 + [one] * 8
     down_t, up, value = pl.pallas_call(
         functools.partial(main_kernel, seqs, dps),
         out_shape=[shape((ch, width), BF16), shape((rank, heads), BF16), shape((1, 1), F32)],

time: 140 us -> 132 us (0.943)
  Pallas kernels: 131 us -> 123 us
    pallas_call x1, Pallas kernels: 131 us -> 123 us  [on_device(): pl.pallas_call(functools.partial(main_kernel, seqs, dps), out_shape=[shap...]
where the time goes in v5:
time: 132 us; the launch traced here: 131 us
  Pallas kernels  123 us (93%)
  other arithmetic  4.33 us (3%)
  between operations  3.7 us (3%)
    pallas_call x1, Pallas kernels, on_device(): pl.pallas_call(functools.partial(main_kernel, seqs, dps), out_shape=[shap...  123 us
    convert_element_type x2, other arithmetic, on_device(): return (down_t.T.astype(F32), up.astype(F32), value.reshape(1))  3.7 us

profile of v5, /device:TPU:1, one launch (start us, length us, event | category | flops | bytes accessed | tf_op | source)
XLA Modules:
  0.0 131.3 jit_solution(8545518826492140495)
XLA Ops:
  1.9 0.1 convert_bitcast_fusion.1
  2.0 0.6 pad_maximum_fusion.emb
  2.6 123.3 %shard_map.166 = (bf16[64,3072]{1,0:T(8,128)(2,1)}, bf16[64,2048]{1,0:T(8,128)(2,1)}, f32[1,1]{1,0:T(1,128)}) custom-call(s32[1]{0:T(128)S(6)} %copy.19.step, s32[1]{0:T(128)S(6)} %copy.20.pref, bf16[1,256]{1,0:T(2,128)(2,1)} %pad_maximum_fusion.emb, bf16[64,96]{1,0:T(8,128)(2,1)} %bitcast.26, bf16[64,96]{1,0:T(8,128)(2,1)} %bitcast.27, ...), custom_call_target="tpu_custom_call" | custom-call | tf_op jit(solution)/shard_map/pallas_call | solution.py:825
  125.9 1.9 %convert_bitcast_fusion = f32[3072,64]{0,1:T(8,128)} fusion(bf16[64,3072]{1,0:T(8,128)(2,1)} %get-tuple-element.6), kind=kLoop, calls=%fused_computation | loop fusion | flops 196608 | bytes 1179648 | tf_op jit(solution)/shard_map/convert_element_type | solution.py:855
  127.8 1.8 %convert_element_type.27 = f32[64,2048]{1,0:T(8,128)} convert(bf16[64,2048]{1,0:T(8,128)(2,1)} %get-tuple-element.7) | non-fusion elementwise | flops 131072 | bytes 786432 | tf_op jit(solution)/shard_map/convert_element_type | solution.py:855

commit v6 on v5

--- a/solution.py
+++ b/solution.py
@@ -315,8 +315,10 @@
     ring_first(0)
     others(me, seqs, lambda peer: noisy_copy(me, peer).start())
     ring_flip(1)
+    ring_first(1)
     mod[:, at_lanes(me * part, part)] = mod_part
     ring_hop(0, 1)
+    ring_hop(1, 1)
 
     mod_others = mod.at[:, pl.ds(0, (seqs - 1) * part)]
     arrived(mod_others, mod_r.at[0], at(seq=flip))
@@ -342,8 +344,6 @@
     score_scale = math.log2(math.e) / math.sqrt(128.0)
     if hops > 1:
         ring_hop(0, 2)
-    ring_first(1)
-    ring_hop(1, 1)
 
     noisy_others = noisy.at[pl.ds(0, seqs - 1)]
     arrived(noisy_others, noi_r.at[0], at(seq=flip))

time: 132 us -> 133 us (level)
  Pallas kernels: 123 us -> 125 us
    pallas_call x1, Pallas kernels: 123 us -> 125 us  [on_device(): pl.pallas_call(functools.partial(main_kernel, seqs, dps), out_shape=[shap...]
where the time goes in v6:
time: 133 us
  Pallas kernels  125 us (94%)
  other arithmetic  4.33 us (3%)
  between operations  3.7 us (3%)
    pallas_call x1, Pallas kernels, on_device(): pl.pallas_call(functools.partial(main_kernel, seqs, dps), out_shape=[shap...  125 us
    convert_element_type x2, other arithmetic, on_device(): return (down_t.T.astype(F32), up.astype(F32), value.reshape(1))  3.7 us

profile of v6, /device:TPU:1, one launch (start us, length us, event | category | flops | bytes accessed | tf_op | source)
XLA Modules:
  0.0 132.8 jit_solution(14825157479936588315)
XLA Ops:
  1.9 0.1 convert_bitcast_fusion.1
  2.0 0.6 pad_maximum_fusion.emb
  2.6 124.8 %shard_map.166 = (bf16[64,3072]{1,0:T(8,128)(2,1)}, bf16[64,2048]{1,0:T(8,128)(2,1)}, f32[1,1]{1,0:T(1,128)}) custom-call(s32[1]{0:T(128)S(6)} %copy.19.step, s32[1]{0:T(128)S(6)} %copy.20.pref, bf16[1,256]{1,0:T(2,128)(2,1)} %pad_maximum_fusion.emb, bf16[64,96]{1,0:T(8,128)(2,1)} %bitcast.26, bf16[64,96]{1,0:T(8,128)(2,1)} %bitcast.27, ...), custom_call_target="tpu_custom_call" | custom-call | tf_op jit(solution)/shard_map/pallas_call | solution.py:825
  127.3 1.9 %convert_bitcast_fusion = f32[3072,64]{0,1:T(8,128)} fusion(bf16[64,3072]{1,0:T(8,128)(2,1)} %get-tuple-element.6), kind=kLoop, calls=%fused_computation | loop fusion | flops 196608 | bytes 1179648 | tf_op jit(solution)/shard_map/convert_element_type | solution.py:855
  129.2 1.8 %convert_element_type.27 = f32[64,2048]{1,0:T(8,128)} convert(bf16[64,2048]{1,0:T(8,128)(2,1)} %get-tuple-element.7) | non-fusion elementwise | flops 131072 | bytes 786432 | tf_op jit(solution)/shard_map/convert_element_type | solution.py:855
